TPU v7x, 256 devices: a whole 4x4x8 slice. The times are simulated.
256 devices in a mesh: section: 64 (over y, x, z_hi, core), tensor: 4 (over z_lo).
Axes of the slice: x: 4, y: 4, z: 8 (z_hi: 2, z_lo: 4; z = z_hi * 4 + z_lo), core: 2. Of those that a mesh axis runs over, the one named last changes fastest.
Arguments:
- fwd_in: bfloat16 [64, 256, 2048], P('section', None, 'tensor'), may hold values from -24 to 24
- bwd_in: bfloat16 [64, 256, 2048], P('section', None, 'tensor'), may hold values from -24 to 24
- cotangent: bfloat16 [64, 256, 2048], P('section', None, 'tensor'), may hold values from -6 to 6
- enc_saved: bfloat16 [256, 2048], P(None, 'tensor'), may hold values from -24 to 24
- norm_gain: bfloat16 [64, 2048], P('section', 'tensor'), may hold values from 0.099609375 to 1.8984375
- final_gain: bfloat16 [2048], P('tensor'), may hold values from 0.099609375 to 1.8984375
- w_qkv: bfloat16 [64, 2048, 3, 2048], P('section', None, None, 'tensor'), may hold values from -0.125 to 0.125
- w_out: bfloat16 [64, 2048, 2048], P('section', 'tensor'), may hold values from -0.375 to 0.375
Outputs:
- fwd_out: bfloat16 [64, 256, 2048], P('section', None, 'tensor')
- grad_in: bfloat16 [64, 256, 2048], P('section', None, 'tensor')
All inputs are finite; a program needn't handle non-finite values.
Results may differ from a plain program's by a relative error of at most 0.017.
Values may be sent and summed in bfloat16 or wider, within the bound.
No kernel may reach another device: no remote copies, remote signals or barrier semaphores. Data moves between devices by JAX's collectives and lax.ppermute only.
A program may use at most 128 MiB of HBM per device.

v0:
```python
import jax
import jax.numpy as jnp
from jax import lax
from jax.sharding import PartitionSpec as P

HEAD_DIM = 256


epsilon = 1e-06


def broadcast(value, axis, root):
    mine = lax.axis_index(axis) == root
    return lax.psum(jnp.where(mine, value, jnp.zeros_like(value)), axis)


def from_behind(value, axis, by):
    peers = lax.axis_size(axis)
    return lax.ppermute(value, axis, [(i, (i + by) % peers) for i in range(peers)])


def inverse_rms(values):
    return lax.rsqrt(jnp.mean(values * values, axis=-1, keepdims=True) + epsilon)


def normalize(values, gain_row):
    return (values * inverse_rms(values) * gain_row.astype(jnp.float32)).astype(jnp.bfloat16)


def head_split(matrix):
    return matrix.reshape(matrix.shape[0], matrix.shape[1] // HEAD_DIM, HEAD_DIM)


def project_source(source, w_key, w_value):
    key_rows = jnp.dot(source, w_key, preferred_element_type=jnp.float32).astype(jnp.bfloat16)
    value_rows = jnp.dot(source, w_value, preferred_element_type=jnp.float32).astype(jnp.bfloat16)
    return (key_rows, value_rows)


def softmax_rows(queries, key_rows):
    scores = jnp.einsum(
        "qhd,khd->hqk",
        head_split(queries),
        head_split(key_rows),
        preferred_element_type=jnp.float32,
    )
    weights = jnp.exp(scores * HEAD_DIM ** (-0.5))
    return weights / jnp.sum(weights, axis=-1, keepdims=True)


def attend_out(queries, source, w_key, w_value, w_proj):
    key_rows, value_rows = project_source(source, w_key, w_value)
    weights = softmax_rows(queries, key_rows)
    mixed_rows = jnp.einsum(
        "hqk,khd->qhd",
        weights.astype(jnp.bfloat16),
        head_split(value_rows),
        preferred_element_type=jnp.float32,
    )
    mixed_rows = mixed_rows.astype(jnp.bfloat16).reshape(queries.shape)
    return jnp.dot(mixed_rows, w_proj, preferred_element_type=jnp.float32)


def attend_back(queries, source, upstream, w_query, w_key, w_value, w_proj):
    key_rows, value_rows = project_source(source, w_key, w_value)
    weights = softmax_rows(queries, key_rows)
    grad_mix = jnp.einsum("rd,cd->rc", upstream, w_proj, preferred_element_type=jnp.float32).astype(
        jnp.bfloat16
    )
    grad_heads = head_split(grad_mix)
    grad_values = jnp.einsum(
        "hqk,qhd->khd", weights.astype(jnp.bfloat16), grad_heads, preferred_element_type=jnp.float32
    )
    grad_values = grad_values.astype(jnp.bfloat16).reshape(queries.shape)
    grad_weights = jnp.einsum(
        "qhd,khd->hqk", grad_heads, head_split(value_rows), preferred_element_type=jnp.float32
    )
    grad_scores = (
        weights
        * (grad_weights - jnp.sum(weights * grad_weights, axis=-1, keepdims=True))
        * HEAD_DIM ** (-0.5)
    )
    grad_scores = grad_scores.astype(jnp.bfloat16)
    grad_query = jnp.einsum(
        "hqk,khd->qhd", grad_scores, head_split(key_rows), preferred_element_type=jnp.float32
    )
    grad_query = grad_query.astype(jnp.bfloat16).reshape(queries.shape)
    grad_keys = jnp.einsum(
        "hqk,qhd->khd", grad_scores, head_split(queries), preferred_element_type=jnp.float32
    )
    grad_keys = grad_keys.astype(jnp.bfloat16).reshape(queries.shape)
    query_term = jnp.einsum("rc,dc->rd", grad_query, w_query, preferred_element_type=jnp.float32)
    source_term = jnp.einsum("rc,dc->rd", grad_keys, w_key, preferred_element_type=jnp.float32)
    source_term = source_term + jnp.einsum(
        "rc,dc->rd", grad_values, w_value, preferred_element_type=jnp.float32
    )
    return (query_term, source_term)


def final_backward(saved, gain_row, gradients):
    inputs = saved.astype(jnp.float32)
    inverse = inverse_rms(inputs)
    scaled_grad = gain_row.astype(jnp.float32) * gradients
    return inverse * scaled_grad - inputs * inverse**3 * jnp.mean(
        scaled_grad * inputs, axis=-1, keepdims=True
    )


def body(fwd_in, bwd_in, cotangent, enc_saved, norm_gain, final_gain, w_qkv, w_out):
    section_count = lax.axis_size("section")
    enc_sections = section_count // 2
    section_index = lax.axis_index("section")
    part_index = lax.axis_index("tensor")
    is_decoder = section_index >= enc_sections
    last_encoder = section_index == enc_sections - 1
    row_count = fwd_in.shape[1]
    shard_width = fwd_in.shape[2]
    fwd_rows, bwd_rows, saved_rows, upstream_rows, gain_full, final_full = (
        lax.all_gather(fwd_in[0], "tensor", axis=1, tiled=True),
        lax.all_gather(bwd_in[0], "tensor", axis=1, tiled=True),
        lax.all_gather(enc_saved, "tensor", axis=1, tiled=True),
        lax.all_gather(cotangent[0], "tensor", axis=1, tiled=True),
        lax.all_gather(norm_gain[0], "tensor", axis=0, tiled=True),
        lax.all_gather(final_gain, "tensor", axis=0, tiled=True),
    )
    full_width = fwd_rows.shape[1]
    weights_in = w_qkv[0]
    w_query = weights_in[:, 0]
    w_key = weights_in[:, 1]
    w_value = weights_in[:, 2]
    w_proj = w_out[0]

    def zero_term(operands):
        return jnp.zeros((row_count, full_width), jnp.float32)

    def zero_pair(operands):
        return (
            jnp.zeros((row_count, full_width), jnp.float32),
            jnp.zeros((row_count, full_width), jnp.float32),
        )

    def attend_local(operands):
        return attend_out(operands[0], operands[1], w_key, w_value, w_proj)

    normed = normalize(fwd_rows.astype(jnp.float32), gain_full)
    queries = jnp.dot(normed, w_query, preferred_element_type=jnp.float32).astype(jnp.bfloat16)
    self_term = lax.cond(is_decoder, zero_term, attend_local, (queries, normed))
    self_out = lax.psum_scatter(
        self_term.astype(jnp.bfloat16), "tensor", scatter_dimension=1, tiled=True
    ).astype(jnp.float32)
    residual = fwd_in[0].astype(jnp.float32)
    encoder_y = (residual + self_out).astype(jnp.bfloat16)
    top_shard = broadcast(encoder_y, "section", enc_sections - 1)
    top_rows = lax.all_gather(top_shard, "tensor", axis=1, tiled=True)
    top_normed = normalize(top_rows.astype(jnp.float32), final_full)
    cross_term = lax.cond(is_decoder, attend_local, zero_term, (queries, top_normed))
    cross_out = lax.psum_scatter(
        cross_term.astype(jnp.bfloat16), "tensor", scatter_dimension=1, tiled=True
    ).astype(jnp.float32)
    decoder_y = (residual + cross_out).astype(jnp.bfloat16)
    layer_out = jnp.where(is_decoder, decoder_y, encoder_y)
    arrived = from_behind(layer_out, "section", 1)
    fwd_out = jnp.where(section_index == enc_sections, jnp.zeros_like(arrived), arrived)[None]
    back_inputs = bwd_rows.astype(jnp.float32)
    back_normed = normalize(back_inputs, gain_full)
    back_queries = jnp.dot(back_normed, w_query, preferred_element_type=jnp.float32).astype(
        jnp.bfloat16
    )
    saved_normed = normalize(saved_rows.astype(jnp.float32), final_full)

    def decoder_back(operands):
        query_term, source_term = attend_back(
            operands[0], operands[1], operands[2], w_query, w_key, w_value, w_proj
        )
        return (query_term, final_backward(saved_rows, final_full, source_term))

    dec_query_term, returned_term = lax.cond(
        is_decoder, decoder_back, zero_pair, (back_queries, saved_normed, upstream_rows)
    )
    returned_full = lax.psum(returned_term, ("section", "tensor")).astype(jnp.bfloat16)
    upstream_full = jnp.where(last_encoder, returned_full, upstream_rows)
    returned_shard = lax.dynamic_slice_in_dim(
        returned_full, part_index * shard_width, shard_width, 1
    )
    upstream_shard = jnp.where(last_encoder, returned_shard, cotangent[0])

    def encoder_back(operands):
        query_term, source_term = attend_back(
            operands[0], operands[1], operands[2], w_query, w_key, w_value, w_proj
        )
        return query_term + source_term

    enc_term = lax.cond(
        is_decoder, zero_term, encoder_back, (back_queries, back_normed, upstream_full)
    )
    grad_term = dec_query_term + enc_term
    inputs_shard = bwd_in[0].astype(jnp.float32)
    gain_shard = norm_gain[0].astype(jnp.float32)
    grad_norm = lax.psum_scatter(
        grad_term.astype(jnp.bfloat16), "tensor", scatter_dimension=1, tiled=True
    ).astype(jnp.float32)
    local_sum = jnp.sum(gain_shard * grad_norm * inputs_shard, axis=-1, keepdims=True)
    row_sum = lax.psum(local_sum, "tensor")
    inverse = inverse_rms(back_inputs)
    scaled_grad = gain_shard * grad_norm
    grad_rows = (
        upstream_shard.astype(jnp.float32)
        + inverse * scaled_grad
        - inputs_shard * inverse**3 * (row_sum / full_width)
    )
    grad_in = grad_rows.astype(jnp.bfloat16)[None]
    return (fwd_out, grad_in)


def solution(mesh):
    in_specs = (
        P("section", None, "tensor"),
        P("section", None, "tensor"),
        P("section", None, "tensor"),
        P(None, "tensor"),
        P("section", "tensor"),
        P("tensor"),
        P("section", None, None, "tensor"),
        P("section", "tensor", None),
    )
    out_specs = (P("section", None, "tensor"), P("section", None, "tensor"))
    return jax.shard_map(body, mesh=mesh, in_specs=in_specs, out_specs=out_specs, check_vma=False)
```

profile of v0, /device:TPU:24, one launch (start us, length us, event | category | flops | bytes accessed | tf_op | source)
XLA Modules:
  0.0 1180.8 jit_solution(2600737513652178894)
XLA Ops:
  7.2 0.7 all-gather.17.cloned.1.call-update
  7.9 0.7 all-gather.15.cloned.1.call-update
  8.7 12.9 %all-gather.1 = bf16[1,2048]{1,0:T(2,128)(2,1)S(1)} all-gather(bf16[1,512]{1,0:T(2,128)(2,1)} %param.20), channel_id=3, replica_groups=mesh['section'=64,'tensor'=4] {'tensor'}, dimensions={1}, use_global_device_ids=true | all-gather | bytes 5120 | tf_op jit(solution)/shard_map/all_gather | solution.py:123
  21.6 5.3 slice_bitcast_fusion
  27.0 19.1 %all-gather.17.cloned.1.call-done = bf16[1,256,2048]{2,1,0:T(8,128)(2,1)} async-done(((bf16[1,256,512]{2,1,0:T(8,128)(2,1)}), bf16[1,256,2048]{2,1,0:T(8,128)(2,1)}) %all-gather.17.cloned.1.call-update) | async-done | bytes 1048592 | tf_op jit(solution)/shard_map/all_gather | solution.py:120
  46.1 1.6 fusion.97
  47.7 32.8 %all-gather.15.cloned.1.call-done = bf16[1,256,2048]{2,1,0:T(8,128)(2,1)} async-done(((bf16[1,256,512]{2,1,0:T(8,128)(2,1)}), bf16[1,256,2048]{2,1,0:T(8,128)(2,1)}) %all-gather.15.cloned.1.call-update) | async-done | bytes 1048592 | tf_op jit(solution)/shard_map/all_gather | solution.py:119
  80.4 1.5 fusion.94
  82.0 2.7 fusion.99
  84.7 3.1 convolution_convert_fusion.19
  87.8 0.1 conditional.4
  87.8 0.1 broadcast.119
  88.0 1.0 copy-done.3
  88.9 0.0 all-reduce.3.cloned.1.call-start
  89.0 39.0 %reduce-scatter.4.cloned.1.call-done = bf16[256,512]{1,0:T(8,128)(2,1)} async-done(((bf16[256,2048]{1,0:T(8,128)(2,1)}), bf16[256,512]{1,0:T(8,128)(2,1)}) %reduce-scatter.4.cloned.1.call-update) | async-done | bytes 262160 | tf_op jit(solution)/shard_map/reduce_scatter | solution.py:148
  128.0 1.7 broadcast_select_fusion
  129.8 0.0 all-gather.13.cloned.1.call-start
  129.8 0.5 all-gather.13.cloned.1.call-update
  130.4 701.9 %all-reduce.3.cloned.1.call-done = bf16[256,512]{1,0:T(8,128)(2,1)} async-done(((bf16[256,512]{1,0:T(8,128)(2,1)}), bf16[256,512]{1,0:T(8,128)(2,1)}) %all-reduce.3.cloned.1.call-update) | async-done | bytes 262160 | tf_op jit(solution)/shard_map/psum | solution.py:14
  832.4 0.7 all-gather.19.cloned.1.call-update
  833.2 12.0 %all-gather.4 = bf16[4,1,512]{2,1,0:T(2,128)(2,1)S(1)} all-gather(bf16[1,1,512]{2,1,0:T(2,128)(2,1)S(1)} %reshape.149), channel_id=1, replica_groups=mesh['section'=64,'tensor'=4] {'tensor'}, dimensions={0}, use_global_device_ids=true | all-gather | bytes 5120 | tf_op jit(solution)/shard_map/all_gather | solution.py:124
  845.3 55.4 %all-gather.13.cloned.1.call-done = bf16[256,2048]{1,0:T(8,128)(2,1)} async-done(((bf16[256,512]{1,0:T(8,128)(2,1)}), bf16[256,2048]{1,0:T(8,128)(2,1)}) %all-gather.13.cloned.1.call-update) | async-done | bytes 1048592 | tf_op jit(solution)/shard_map/all_gather | solution.py:121
  900.7 1.6 fusion.91
  902.3 32.6 %all-gather.11.cloned.1.call-done = bf16[256,2048]{1,0:T(8,128)(2,1)} async-done(((bf16[256,512]{1,0:T(8,128)(2,1)}), bf16[256,2048]{1,0:T(8,128)(2,1)}) %all-gather.11.cloned.1.call-update) | async-done | bytes 1048592 | tf_op jit(solution)/shard_map/all_gather | solution.py:154
  934.9 1.5 fusion.88
  936.5 3.1 fusion.93
  939.6 15.5 %conditional.5 = (bf16[256,2048]{1,0:T(8,128)(2,1)}) conditional(s32[]{:T(128)} %convert_element_type.188, () %tuple.34, (bf16[256,2048]{1,0:T(8,128)(2,1)}, bf16[2048,512]{1,0:T(8,128)(2,1)}, bf16[2048,512]{1,0:T(8,128)(2,1)}, bf16[256,512]{1,0:T(8,128)(2,1)}, bf16[512,2048]{1,0:T(8,128)(2,1)}) %tuple.87), branch_computations={%region_7.8_spmd, %region_8.10_spmd} | conditional | flops 1745617664 | bytes 12845064 | solution.py:156
  939.6 3.3 convolution_convert_fusion.5
  942.9 1.8 copy.111
  944.7 2.6 convolution_convert_fusion.4
  947.3 2.0 fusion.16
  949.4 2.3 convolution_convert_fusion.3
  951.6 3.4 fusion.109
  955.1 0.0 reduce-scatter.8.cloned.1.call-start
  955.1 3.4 convolution_convert_fusion.18
  958.5 10.8 all-gather.19.cloned.1.call-done
  969.3 38.5 %conditional.6 = (f32[256,2048]{1,0:T(8,128)}, f32[256,2048]{1,0:T(8,128)}) conditional(s32[]{:T(128)} %convert_element_type.188, () %tuple.38, (bf16[256,2048]{1,0:T(8,128)(2,1)}, bf16[2048,512]{1,0:T(8,128)(2,1)}, bf16[256,512]{1,0:T(8,128)(2,1)}, bf16[256,2048]{1,0:T(8,128)(2,1)}, bf16[512,2048]{1,0:T(8,128)(2,1)}, ...), branch_computations={%region_13.14_spmd, %region_14.19_spmd} | conditional | flops 3632928512 | bytes 44071012 | solution.py:177
  969.3 3.3 convolution_convert_fusion.11
  972.6 1.8 copy.112
  974.4 1.8 copy.98
  976.2 2.2 fusion.51
  978.4 3.4 convolution_convert_fusion.10
  981.7 1.8 copy.113
  983.6 2.7 convolution_convert_fusion.9
  986.2 1.1 fusion.46
  987.3 2.6 convolution_convert_fusion.8
  989.9 3.0 fusion.110
  992.9 2.6 convolution_convert_fusion.7
  995.5 3.9 fusion.111
  999.4 1.1 fusion.40
  1000.5 2.3 convolution_convert_fusion.6
  1002.8 3.2 fusion.32
  1006.0 1.8 fusion.34
  1007.8 82.8 %all-reduce.4 = bf16[256,2048]{1,0:T(8,128)(2,1)S(1)} all-reduce(f32[256,2048]{1,0:T(8,128)} %get-tuple-element.99), channel_id=1, replica_groups=mesh['section'=64,'tensor'=4] {'section','tensor'}, use_global_device_ids=true, to_apply=%region_19.20 | all-reduce | flops 524288 | bytes 3145728 | tf_op jit(solution)/shard_map/psum | solution.py:180
  1090.6 1.9 conditional.7
  1090.9 1.6 broadcast.127
  1092.5 3.5 add_convert_fusion
  1096.1 1.1 fusion.107
  1097.3 1.9 collective-permute-start
  1099.2 62.1 %reduce-scatter.8.cloned.1.call-done = bf16[256,512]{1,0:T(8,128)(2,1)} async-done(((bf16[256,2048]{1,0:T(8,128)(2,1)}), bf16[256,512]{1,0:T(8,128)(2,1)}) %reduce-scatter.8.cloned.1.call-update) | async-done | bytes 262160 | tf_op jit(solution)/shard_map/reduce_scatter | solution.py:199
  1161.2 1.1 fusion.105
  1162.4 9.3 psum.23
  1171.7 1.9 fusion.106
  1173.5 0.7 select_bitcast_fusion
  (51 shorter events, 0.5 us)
Async XLA Ops:
  7.2 38.9 %all-gather.17.cloned.1.call-start = ((), (), s32[]{:S(2)}) async-start(), calls=%async_computation.10 | async-start | bytes 1310720 | tf_op jit(solution)/shard_map/all_gather | solution.py:120
  7.9 72.5 %all-gather.15.cloned.1.call-start = ((), (), s32[]{:S(2)}) async-start(), calls=%async_computation.9 | async-start | bytes 1310720 | tf_op jit(solution)/shard_map/all_gather | solution.py:119
  8.6 119.4 %reduce-scatter.4.cloned.1.call-start = ((), (), s32[]{:S(2)}) async-start(), calls=%async_computation.3 | async-start | bytes 1310720 | tf_op jit(solution)/shard_map/reduce_scatter | solution.py:148
  46.1 35.9 %copy-start.4 = (bf16[1,256,2048]{2,1,0:T(8,128)(2,1)S(1)}, bf16[1,256,2048]{2,1,0:T(8,128)(2,1)}, u32[]{:S(2)}) copy-start(bf16[1,256,2048]{2,1,0:T(8,128)(2,1)} %all-gather.17.cloned.1.call-done) | copy-start | bytes 3145732
  84.7 3.2 copy-start
  87.8 40.2 %copy-start.6 = (bf16[1,256,512]{2,1,0:T(8,128)(2,1)S(1)}, bf16[1,256,512]{2,1,0:T(8,128)(2,1)}, u32[]{:S(2)}) copy-start(bf16[1,256,512]{2,1,0:T(8,128)(2,1)} %param.16) | copy-start | bytes 786436
  87.9 1.0 copy-start.3
  87.9 745.2 %copy-start.17 = (bf16[512]{0:T(512)(128)(2,1)S(1)}, bf16[512]{0:T(512)(128)(2,1)}, u32[]{:S(2)}) copy-start(bf16[512]{0:T(512)(128)(2,1)} %param.21) | copy-start | bytes 3076
  88.9 743.4 %all-reduce.3.cloned.1.call-start = ((), (), s32[]{:S(2)}) async-start(), calls=%async_computation.4 | async-start | bytes 524288 | tf_op jit(solution)/shard_map/psum | solution.py:14
  129.8 770.9 %all-gather.13.cloned.1.call-start = ((), (), s32[]{:S(2)}) async-start(), calls=%async_computation.7 | async-start | bytes 1310720 | tf_op jit(solution)/shard_map/all_gather | solution.py:121
  130.3 804.6 %all-gather.11.cloned.1.call-start = ((), (), s32[]{:S(2)}) async-start(), calls=%async_computation.5 | async-start | bytes 1310720 | tf_op jit(solution)/shard_map/all_gather | solution.py:154
  832.4 137.0 %all-gather.19.cloned.1.call-start = ((), (), s32[]{:S(2)}) async-start(), calls=%async_computation.11 | async-start | bytes 1310720 | tf_op jit(solution)/shard_map/all_gather | solution.py:122
  833.1 263.0 %reduce-scatter.6.cloned.1.call-start = ((), (), s32[]{:S(2)}) async-start(), calls=%async_computation.6 | async-start | bytes 1310720 | tf_op jit(solution)/shard_map/reduce_scatter | solution.py:157
  900.7 35.8 %copy-start.2 = (bf16[256,2048]{1,0:T(8,128)(2,1)S(1)}, bf16[256,2048]{1,0:T(8,128)(2,1)}, u32[]{:S(2)}) copy-start(bf16[256,2048]{1,0:T(8,128)(2,1)} %all-gather.13.cloned.1.call-done) | copy-start | bytes 3145732
  955.1 206.2 %reduce-scatter.8.cloned.1.call-start = ((), (), s32[]{:S(2)}) async-start(), calls=%async_computation.8 | async-start | bytes 1310720 | tf_op jit(solution)/shard_map/reduce_scatter | solution.py:199
  983.5 2.7 copy-start.12
  995.5 3.9 copy-start.8
  995.5 3.9 copy-start.10
  1092.5 3.6 copy-start.16
  1092.5 3.6 copy-start.15
  1096.0 65.2 %copy-start.5 = (bf16[1,256,512]{2,1,0:T(8,128)(2,1)S(1)}, bf16[1,256,512]{2,1,0:T(8,128)(2,1)}, u32[]{:S(2)}) copy-start(bf16[1,256,512]{2,1,0:T(8,128)(2,1)} %param.17) | copy-start | bytes 786436
  1096.0 75.6 %copy-start.7 = (bf16[1,256,512]{2,1,0:T(8,128)(2,1)S(1)}, bf16[1,256,512]{2,1,0:T(8,128)(2,1)}, u32[]{:S(2)}) copy-start(bf16[1,256,512]{2,1,0:T(8,128)(2,1)} %param.18) | copy-start | bytes 786436
  1097.3 76.3 %collective-permute-start = (bf16[256,512]{1,0:T(8,128)(2,1)S(1)}, bf16[256,512]{1,0:T(8,128)(2,1)S(1)}, u32[]{:S(2)}, u32[]{:S(2)}) collective-permute-start(bf16[256,512]{1,0:T(8,128)(2,1)S(1)} %fusion.107), channel_id=1, source_target_pairs={{0,4},{4,8},{8,12},{12,16},{16,20},{20,24},{24,28},{28,32},{32,36}... | collective-permute-start | bytes 786440 | tf_op jit(solution)/shard_map/ppermute | solution.py:19
Sparse Core Ops, SparseCore 0:
  9.8 36.2 all-gather.16
  47.9 32.5 all-gather.14
  89.1 38.8 reduce-scatter.3
  131.2 701.0 all-reduce.2
  834.0 66.6 all-gather.12
  902.4 32.5 all-gather.10
  936.7 32.5 all-gather.18
  971.9 31.4 reduce-scatter.5
  1096.2 65.0 reduce-scatter.7
where the time goes:
time: 1180 us
  waiting for transfers between devices  956 us (81%)
  blocking collectives  117 us (10%)
  matrix products  51.4 us (4%)
  other arithmetic  24 us (2%)
  local copies, waits for them, and re-layouts  15.3 us (1%)
  between operations  14 us (1%)
    psum x1, waiting for transfers between devices, broadcast(): return lax.psum(jnp.where(mine, value, jnp.zeros_like(value)), axis)  702 us
    psum x1, blocking collectives, body(): lax.psum(returned_term, ('section', 'tensor')).astype(jnp.bfloat16)  82.8 us
    reduce_scatter x1, waiting for transfers between devices, body(): lax.psum_scatter(grad_term.astype(jnp.bfloat16), 'tensor', scatter_dimens...  62.1 us
    all_gather x1, waiting for transfers between devices, body(): lax.all_gather(enc_saved, 'tensor', axis=1, tiled=True)  55.4 us
    reduce_scatter x1, waiting for transfers between devices, body(): lax.psum_scatter(self_term.astype(jnp.bfloat16), 'tensor', scatter_dimens...  39 us
    all_gather x1, waiting for transfers between devices, body(): lax.all_gather(fwd_in[0], 'tensor', axis=1, tiled=True)  32.8 us
    all_gather x1, waiting for transfers between devices, body(): top_rows = lax.all_gather(top_shard, 'tensor', axis=1, tiled=True)  32.6 us
  transfers between devices with their start and end apart: 10, of which 8 were waited for; matrix products, arithmetic and copies ran while one was open for 7% of the time, Pallas kernels for 0%

commit v1 on v0

v1 whole, which is shorter than its diff:
```python
import jax
import jax.numpy as jnp
from jax import lax
from jax.sharding import PartitionSpec as P

HEAD_DIM = 256
NY, NX, NZ, NC, NT = 4, 4, 2, 2, 4
SECTION_COUNT = NY * NX * NZ * NC
ENC_SECTIONS = SECTION_COUNT // 2
LAST = ENC_SECTIONS - 1

epsilon = 1e-06
f32 = jnp.float32
bf16 = jnp.bfloat16

PLACES = [
    (y, x, z, c, t)
    for y in range(NY)
    for x in range(NX)
    for z in range(NZ)
    for c in range(NC)
    for t in range(NT)
]


def place_index(place):
    y, x, z, c, t = place
    return (((y * NX + x) * NZ + z) * NC + c) * NT + t


def section_of(place):
    return place_index(place) // NT


def move(value, route):
    pairs = []
    for place in PLACES:
        target = route(*place)
        if target is not None:
            pairs.append((place_index(place), place_index(target)))
    return lax.ppermute(value, ("section", "tensor"), pairs)


def ring_slots(value, axis, size, only=None):
    def route(step):
        def go(*place):
            target = list(place)
            target[axis] = (place[axis] - step) % size
            if only is not None and not only(*target):
                return None
            return tuple(target)

        return go

    return [value] + [move(value, route(step)) for step in range(1, size)]


def line_gather(shard):
    right, left = shard, shard
    from_left, from_right = [], []
    for step in range(1, NT):
        right = move(right, lambda y, x, z, c, t: (y, x, z, c, t + 1) if step - 1 <= t < NT - 1 else None)
        left = move(left, lambda y, x, z, c, t: (y, x, z, c, t - 1) if 0 < t <= NT - step else None)
        from_left.append(right)
        from_right.append(left)
    t = lax.axis_index("tensor")
    slots = [shard]
    for k in range(1, NT):
        slots.append(jnp.where(t + k < NT, from_right[k - 1], from_left[NT - k - 1]))
    return jnp.concatenate(slots, axis=1)


def line_scatter(total):
    width = total.shape[1] // NT
    chunk = lambda k: total[:, k * width : (k + 1) * width].astype(f32)
    from_left = from_right = None
    for step in range(1, NT):
        right, left = chunk(NT - step), chunk(step)
        if step > 1:
            right, left = right + from_left.astype(f32), left + from_right.astype(f32)
        from_left = move(
            right.astype(bf16), lambda y, x, z, c, t: (y, x, z, c, t + 1) if t <= min(step - 1, NT - 2) else None
        )
        from_right = move(
            left.astype(bf16), lambda y, x, z, c, t: (y, x, z, c, t - 1) if t >= max(NT - step, 1) else None
        )
    return chunk(0) + from_left.astype(f32) + from_right.astype(f32)


def row_total(partial):
    rows = partial.shape[0]
    flat = partial.reshape(rows // 128, 128) if rows % 128 == 0 else partial.reshape(1, rows)
    return sum(ring_slots(flat, 4, NT)).reshape(rows, 1)


def inverse_rms(values):
    return lax.rsqrt(jnp.mean(values * values, axis=-1, keepdims=True) + epsilon)


def scale_rows(values, inverse, gain_row):
    return (values * inverse * gain_row).astype(bf16)


def mm(a, b):
    return jnp.dot(a, b, preferred_element_type=f32)


def mm_t(a, b):
    return lax.dot_general(a, b, (((1,), (1,)), ((), ())), preferred_element_type=f32)


def t_mm(a, b):
    return lax.dot_general(a, b, (((0,), (0,)), ((), ())), preferred_element_type=f32)


def heads_of(matrix):
    return [matrix[:, h * HEAD_DIM : (h + 1) * HEAD_DIM] for h in range(matrix.shape[1] // HEAD_DIM)]


def softmax_rows(queries, keys):
    weights = jnp.exp(mm_t(queries, keys) * HEAD_DIM ** (-0.5))
    return weights / jnp.sum(weights, axis=-1, keepdims=True)


def attend_out(q, k, v, w_proj):
    mixed = [
        mm(softmax_rows(qh, kh).astype(bf16), vh).astype(bf16)
        for qh, kh, vh in zip(heads_of(q), heads_of(k), heads_of(v))
    ]
    return mm(jnp.concatenate(mixed, axis=1), w_proj)


def attend_back(q, k, v, upstream, w_proj):
    grad_mix = mm_t(upstream, w_proj).astype(bf16)
    dq, dk, dv = [], [], []
    for qh, kh, vh, gh in zip(heads_of(q), heads_of(k), heads_of(v), heads_of(grad_mix)):
        weights = softmax_rows(qh, kh)
        dv.append(t_mm(weights.astype(bf16), gh).astype(bf16))
        grad_weights = mm_t(gh, vh)
        grad_scores = (
            weights
            * (grad_weights - jnp.sum(weights * grad_weights, axis=-1, keepdims=True))
            * HEAD_DIM ** (-0.5)
        ).astype(bf16)
        dq.append(mm(grad_scores, kh).astype(bf16))
        dk.append(t_mm(grad_scores, qh).astype(bf16))
    return [jnp.concatenate(parts, axis=1) for parts in (dq, dk, dv)]


def is_dec(y):
    return y >= NY // 2


def gather_rows(own):
    half = jnp.concatenate(ring_slots(own, 1, NX), axis=0)
    return jnp.concatenate(ring_slots(half, 3, NC), axis=0)


def body(fwd_in, bwd_in, cotangent, enc_saved, norm_gain, final_gain, w_qkv, w_out):
    section_index = lax.axis_index("section")
    t = lax.axis_index("tensor")
    core = section_index % NC
    x_at = section_index // (NC * NZ) % NX
    y_at = section_index // (NC * NZ * NX)
    dec = section_index >= ENC_SECTIONS
    last = section_index == LAST
    fwd_shard, bwd_shard, cot_shard = fwd_in[0], bwd_in[0], cotangent[0]
    rows, width = fwd_shard.shape
    full = width * NT
    part = rows // (NX * NC)

    a_full = line_gather(jnp.where(dec, bwd_shard, fwd_shard))
    gains = jnp.concatenate([norm_gain, final_gain[None]], axis=0)
    gains = jnp.concatenate(ring_slots(gains, 4, NT), axis=1).astype(f32)
    gain, final = gains[0:1], gains[1:2]
    own_rows = lax.dynamic_slice_in_dim(enc_saved, (x_at * NC + core) * part, part, 0)
    saved = jnp.concatenate(ring_slots(own_rows, 4, NT), axis=1).astype(f32)
    saved_inverse = inverse_rms(saved)
    saved_normed = gather_rows(scale_rows(saved, saved_inverse, final))
    b_full = line_gather(jnp.where(dec, cot_shard, bwd_shard))
    c_full = line_gather(jnp.where(dec, fwd_shard, cot_shard))

    order = [(t + k) % NT for k in range(NT)]
    w_in = w_qkv[0]
    turned = [lax.dynamic_slice_in_dim(w_in, o * width, width, 0) for o in order]
    w_q, w_k, w_v = (jnp.concatenate([w[:, i] for w in turned], axis=0) for i in range(3))
    w_o = jnp.concatenate([lax.dynamic_slice_in_dim(w_out[0], o * width, width, 1) for o in order], axis=1)

    a_values = a_full.astype(f32)
    a_inverse = inverse_rms(a_values)
    a_normed = scale_rows(a_values, a_inverse, gain)
    source = jnp.where(dec, saved_normed, a_normed)
    q1 = mm(a_normed, w_q).astype(bf16)
    k1 = mm(source, w_k).astype(bf16)
    v1 = mm(source, w_v).astype(bf16)

    def dec_back(_):
        dq, dk, dv = attend_back(q1, k1, v1, b_full, w_o)
        return mm_t(dq, w_q).astype(bf16), (mm_t(dk, w_k) + mm_t(dv, w_v)).astype(bf16)

    def enc_forward(_):
        return attend_out(q1, k1, v1, w_o).astype(bf16), jnp.zeros((rows, full), bf16)

    term1, dc = lax.cond(dec, dec_back, enc_forward, 0)

    def dec_only(route):
        return lambda y, x, z, c, tt: route(y, x, z, c, tt) if is_dec(y) else None

    half = rows // NC
    got = move(dc[half:], dec_only(lambda y, x, z, c, tt: (y, x, z, 1 - c, tt)))
    acc = dc[:half].astype(f32) + got.astype(f32)
    acc16 = acc.astype(bf16)
    total = acc[:part]
    for k in range(1, NX):
        total = total + move(
            acc16[k * part : (k + 1) * part], dec_only(lambda y, x, z, c, tt: (y, (x + k) % NX, z, c, tt))
        ).astype(f32)
    low = y_at % 2 == 0
    few = part // 2
    keep = jnp.where(low, total[:few], total[few:])
    give = jnp.where(low, total[few:], total[:few]).astype(bf16)
    keep = keep + move(give, dec_only(lambda y, x, z, c, tt: (y ^ 1, x, z, c, tt))).astype(f32)
    keep16 = keep.astype(bf16)
    mine = keep[:, :width]
    for k in range(1, NT):
        mine = mine + move(
            keep16[:, k * width : (k + 1) * width], dec_only(lambda y, x, z, c, tt: (y, x, z, c, (tt + k) % NT))
        ).astype(f32)
    mine = mine + move(mine, dec_only(lambda y, x, z, c, tt: (y, x, 1 - z, c, tt)))
    u = final * jnp.concatenate(ring_slots(mine, 4, NT, lambda y, x, z, c, tt: is_dec(y)), axis=1)
    e = jnp.where(low, saved[:few], saved[few:])
    r = jnp.where(low, saved_inverse[:few], saved_inverse[few:])
    returned = (r * u - e * r**3 * jnp.mean(u * e, axis=-1, keepdims=True)).astype(bf16)
    to_last = lambda frm: lambda y, x, z, c, tt: (1, x, z, c, tt) if (y == frm and z == 1) else None
    block = jnp.concatenate([move(returned, to_last(2)), move(returned, to_last(3))], axis=0)
    at_last = lambda y, x, z, c, tt: y == 1 and x == NX - 1 and z == 1
    slots = ring_slots(block, 1, NX, at_last)
    other = move(
        jnp.stack(slots), lambda y, x, z, c, tt: (y, x, z, 1, tt) if at_last(y, x, z, c, tt) and c == 0 else None
    )
    pieces = []
    for xi in range(NX):
        k = (xi - (NX - 1)) % NX
        pieces += [other[k], slots[k]]
    returned_full = jnp.concatenate(pieces, axis=0)

    summed1 = line_scatter(term1)
    enc_y = (fwd_shard.astype(f32) + summed1).astype(bf16)

    blocks = enc_y.reshape(NX, NC, part, width)
    is_last = lambda y, x, z, c, tt: section_of((y, x, z, c, tt)) == LAST
    passed = move(blocks[:, 0], lambda y, x, z, c, tt: (y, x, z, 0, tt) if is_last(y, x, z, c, tt) else None)
    blocks = jnp.where(core == 1, blocks[:, 1], passed)
    top = jnp.where(x_at == NX - 1, blocks[NX - 1], jnp.zeros_like(blocks[0]))
    for xi in range(NX - 1):
        top = top + move(
            blocks[xi], lambda y, x, z, c, tt: (y, xi, z, c, tt) if y == 1 and x == NX - 1 and z == 1 else None
        )
    arrivals = [
        move(top, lambda y, x, z, c, tt: (y_to, x, z_to, c, tt) if y == 1 and z == 1 else None)
        for y_to in (2, 3)
        for z_to in (0, 1)
    ]
    top = sum(arrivals)
    top = jnp.concatenate(ring_slots(top, 4, NT, lambda y, x, z, c, tt: is_dec(y)), axis=1).astype(f32)
    top_normed = scale_rows(top, inverse_rms(top), final)
    dec_slots = lambda v, axis, size: ring_slots(v, axis, size, lambda y, x, z, c, tt: is_dec(y))
    top_full = jnp.concatenate(dec_slots(top_normed, 1, NX), axis=0)
    top_full = jnp.concatenate(dec_slots(top_full, 3, NC), axis=0)

    b_values = jnp.where(dec, c_full, b_full).astype(f32)
    b_inverse = inverse_rms(b_values)
    b_normed = scale_rows(b_values, b_inverse, gain)
    q2 = mm(b_normed, w_q).astype(bf16)
    source2 = jnp.where(dec, top_full, b_normed)
    k2 = mm(source2, w_k).astype(bf16)
    v2 = mm(source2, w_v).astype(bf16)
    upstream = jnp.where(last, returned_full, c_full)

    def dec_forward(_):
        return attend_out(q2, k2, v2, w_o).astype(bf16)

    def enc_back(_):
        dq, dk, dv = attend_back(q2, k2, v2, upstream, w_o)
        return (mm_t(dq, w_q) + mm_t(dk, w_k) + mm_t(dv, w_v)).astype(bf16)

    term2 = lax.cond(dec, dec_forward, enc_back, 0)
    summed2 = line_scatter(term2)

    layer_out = jnp.where(dec, (fwd_shard.astype(f32) + summed2).astype(bf16), enc_y)

    def following(y, x, z, c, tt):
        s = section_of((y, x, z, c, tt))
        n = ((s + 1) % SECTION_COUNT) * NT + tt
        return None if s == LAST else PLACES[n]

    fwd_out = move(layer_out, following)[None]

    back_values = jnp.where(dec, a_values, b_values)
    back_term = jnp.where(dec, term1, term2).astype(f32)
    inverse = jnp.where(dec, a_inverse, b_inverse)
    summed = jnp.where(dec, summed1, summed2)
    row_sum = row_total(jnp.sum(gain * back_term * back_values, axis=-1))
    upstream_shard = jnp.where(last, returned_full[:, :width], cot_shard).astype(f32)
    grad_in = (
        upstream_shard
        + inverse * (gain[:, :width] * summed)
        - bwd_shard.astype(f32) * inverse**3 * (row_sum / full)
    ).astype(bf16)[None]
    return (fwd_out, grad_in)


def solution(mesh):
    in_specs = (
        P("section", None, "tensor"),
        P("section", None, "tensor"),
        P("section", None, "tensor"),
        P(None, "tensor"),
        P("section", "tensor"),
        P("tensor"),
        P("section", None, None, "tensor"),
        P("section", "tensor", None),
    )
    out_specs = (P("section", None, "tensor"), P("section", None, "tensor"))
    return jax.shard_map(body, mesh=mesh, in_specs=in_specs, out_specs=out_specs, check_vma=False)
```

time: 1180 us -> 460 us (0.39)
  waiting for transfers between devices: 956 us -> 68 us
  starting transfers between devices: 2.27 us -> 339 us
  blocking collectives: 117 us -> 0 us
  matrix products: 51.4 us -> 12.5 us
    psum x1 -> x0, waiting for transfers between devices: 702 us -> none  [broadcast(): return lax.psum(jnp.where(mine, value, jnp.zeros_like(value)), axis)]
    ppermute x1 -> x77, starting transfers between devices: 1.92 us -> 339 us  [move(): return lax.ppermute(value, ('section', 'tensor'), pairs)]
    all_gather x5 -> x0, waiting for transfers between devices: 151 us -> none  [the longest x1 55.4 us: body(): lax.all_gather(enc_saved, 'tensor', axis=1, tiled=True)]
    reduce_scatter x3 -> x0, waiting for transfers between devices: 101 us -> none  [the longest x1 62.1 us: body(): lax.psum_scatter(grad_term.astype(jnp.bfloat16), 'tensor', scatter_dimens...]
    psum x2 -> x0, blocking collectives: 92.1 us -> none  [the longest x1 82.8 us: body(): lax.psum(returned_term, ('section', 'tensor')).astype(jnp.bfloat16)]
    ppermute x1 -> x77, waiting for transfers between devices: 0.01 us -> 68 us  [move(): return lax.ppermute(value, ('section', 'tensor'), pairs)]
    dot_general x18 -> x25, matrix products: 49.2 us -> 12.5 us  [the longest x11 6.22 us: mm(): return jnp.dot(a, b, preferred_element_type=f32)]
    all_gather x2 -> x0, blocking collectives: 25 us -> none  [the longest x1 12.9 us: body(): lax.all_gather(norm_gain[0], 'tensor', axis=0, tiled=True)]
  transfers between devices with their start and end apart: 10 -> 77, of which waited for: 8 -> 15; matrix products, arithmetic and copies ran while one was open for 7% -> 5% of each run, Pallas kernels for 0% -> 0%
where the time goes in v1:
time: 460 us; the launch traced here: 457 us
  starting transfers between devices  339 us (74%)
  waiting for transfers between devices  68 us (15%)
  local copies, waits for them, and re-layouts  19.3 us (4%)
  other arithmetic  15.8 us (3%)
  matrix products  12.5 us (3%)
    ppermute x77, starting transfers between devices, move(): return lax.ppermute(value, ('section', 'tensor'), pairs)  339 us
    ppermute x77, waiting for transfers between devices, move(): return lax.ppermute(value, ('section', 'tensor'), pairs)  68 us
    unnamed x156, local copies, waits for them, and re-layouts  12.6 us
  transfers between devices with their start and end apart: 77, of which 15 were waited for; matrix products, arithmetic and copies ran while one was open for 5% of the time, Pallas kernels for 0%

profile of v1, /device:TPU:24, one launch (start us, length us, event | category | flops | bytes accessed | tf_op | source)
XLA Modules:
  0.0 457.3 jit_solution(9406956407225315449)
XLA Ops:
  1.6 12.6 %collective-permute-start.21 = (bf16[32,512]{1,0:T(8,128)(2,1)S(1)}, bf16[32,512]{1,0:T(8,128)(2,1)S(1)}, u32[]{:S(2)}, u32[]{:S(2)}) collective-permute-start(bf16[32,512]{1,0:T(8,128)(2,1)S(1)} %constant_dynamic-slice_fusion), channel_id=1, source_target_pairs={{0,3},{1,0},{2,1},{3,2},{4,7},{5,4},{6,5},{7,6},{8,11},{9,8},{10,9... | collective-permute-start | bytes 98312 | tf_op jit(solution)/shard_map/ppermute | solution.py:41
  14.1 11.8 %collective-permute-start.22 = (bf16[32,512]{1,0:T(8,128)(2,1)S(1)}, bf16[32,512]{1,0:T(8,128)(2,1)S(1)}, u32[]{:S(2)}, u32[]{:S(2)}) collective-permute-start(bf16[32,512]{1,0:T(8,128)(2,1)S(1)} %constant_dynamic-slice_fusion), channel_id=1, source_target_pairs={{0,2},{1,3},{2,0},{3,1},{4,6},{5,7},{6,4},{7,5},{8,10},{9,11},{10,... | collective-permute-start | bytes 98312 | tf_op jit(solution)/shard_map/ppermute | solution.py:41
  27.4 4.1 collective-permute-start.12
  32.4 3.2 dynamic-slice_bitcast_fusion.3
  42.5 10.4 %collective-permute-start.23 = (bf16[32,512]{1,0:T(8,128)(2,1)S(1)}, bf16[32,512]{1,0:T(8,128)(2,1)S(1)}, u32[]{:S(2)}, u32[]{:S(2)}) collective-permute-start(bf16[32,512]{1,0:T(8,128)(2,1)S(1)} %constant_dynamic-slice_fusion), channel_id=1, source_target_pairs={{0,1},{1,2},{2,3},{3,0},{4,5},{5,6},{6,7},{7,4},{8,9},{9,10},{10,1... | collective-permute-start | bytes 98312 | tf_op jit(solution)/shard_map/ppermute | solution.py:41
  54.2 15.0 %collective-permute-start.7 = (bf16[256,512]{1,0:T(8,128)(2,1)S(1)}, bf16[256,512]{1,0:T(8,128)(2,1)}, u32[]{:S(2)}, u32[]{:S(2)}) collective-permute-start(bf16[256,512]{1,0:T(8,128)(2,1)S(1)} %get-tuple-element.169), channel_id=1, source_target_pairs={{0,1},{1,2},{2,3},{4,5},{5,6},{6,7},{8,9},{9,10},{10,11},{12,13},{... | collective-permute-start | bytes 786440 | tf_op jit(solution)/shard_map/ppermute | solution.py:41
  70.1 11.8 %collective-permute-start.24 = (bf16[32,2048]{1,0:T(8,128)(2,1)S(1)}, bf16[32,2048]{1,0:T(8,128)(2,1)S(1)}, u32[]{:S(2)}, u32[]{:S(2)}) collective-permute-start(bf16[32,2048]{1,0:T(8,128)(2,1)S(1)} %get-tuple-element.105), channel_id=1, source_target_pairs={{0,48},{1,49},{2,50},{3,51},{4,52},{5,53},{6,54},{7,55},{8,56},{9,... | collective-permute-start | bytes 393224 | tf_op jit(solution)/shard_map/ppermute | solution.py:41
  82.0 11.8 %collective-permute-start.25 = (bf16[32,2048]{1,0:T(8,128)(2,1)S(1)}, bf16[32,2048]{1,0:T(8,128)(2,1)S(1)}, u32[]{:S(2)}, u32[]{:S(2)}) collective-permute-start(bf16[32,2048]{1,0:T(8,128)(2,1)S(1)} %get-tuple-element.105), channel_id=1, source_target_pairs={{0,32},{1,33},{2,34},{3,35},{4,36},{5,37},{6,38},{7,39},{8,40},{9,... | collective-permute-start | bytes 393224 | tf_op jit(solution)/shard_map/ppermute | solution.py:41
  93.8 11.8 %collective-permute-start.26 = (bf16[32,2048]{1,0:T(8,128)(2,1)S(1)}, bf16[32,2048]{1,0:T(8,128)(2,1)S(1)}, u32[]{:S(2)}, u32[]{:S(2)}) collective-permute-start(bf16[32,2048]{1,0:T(8,128)(2,1)S(1)} %get-tuple-element.105), channel_id=1, source_target_pairs={{0,16},{1,17},{2,18},{3,19},{4,20},{5,21},{6,22},{7,23},{8,24},{9,... | collective-permute-start | bytes 393224 | tf_op jit(solution)/shard_map/ppermute | solution.py:41
  105.7 1.6 pad_maximum_fusion.3
  107.3 3.6 collective-permute-start.1
  112.3 13.4 %collective-permute-start.16 = (bf16[256,512]{1,0:T(8,128)(2,1)S(1)}, bf16[256,512]{1,0:T(8,128)(2,1)S(1)}, u32[]{:S(2)}, u32[]{:S(2)}) collective-permute-start(bf16[256,512]{1,0:T(8,128)(2,1)S(1)} %get-tuple-element.168), channel_id=1, source_target_pairs={{0,1},{1,2},{2,3},{4,5},{5,6},{6,7},{8,9},{9,10},{10,11},{12,13},{... | collective-permute-start | bytes 786440 | tf_op jit(solution)/shard_map/ppermute | solution.py:41
  129.0 14.9 %collective-permute-start.8 = (bf16[256,512]{1,0:T(8,128)(2,1)}, bf16[256,512]{1,0:T(8,128)(2,1)S(1)}, u32[]{:S(2)}, u32[]{:S(2)}) collective-permute-start(bf16[256,512]{1,0:T(8,128)(2,1)} %collective-permute-done.7), channel_id=1, source_target_pairs={{1,2},{2,3},{5,6},{6,7},{9,10},{10,11},{13,14},{14,15},{17,18},{18... | collective-permute-start | bytes 786440 | tf_op jit(solution)/shard_map/ppermute | solution.py:41
  144.5 12.5 %collective-permute-start.2 = (bf16[256,512]{1,0:T(8,128)(2,1)S(1)}, bf16[256,512]{1,0:T(8,128)(2,1)S(1)}, u32[]{:S(2)}, u32[]{:S(2)}) collective-permute-start(bf16[256,512]{1,0:T(8,128)(2,1)S(1)} %collective-permute-done.1), channel_id=1, source_target_pairs={{1,2},{2,3},{5,6},{6,7},{9,10},{10,11},{13,14},{14,15},{17,18},{18... | collective-permute-start | bytes 786440 | tf_op jit(solution)/shard_map/ppermute | solution.py:41
  157.1 12.5 %collective-permute-start.4 = (bf16[256,512]{1,0:T(8,128)(2,1)S(1)}, bf16[256,512]{1,0:T(8,128)(2,1)S(1)}, u32[]{:S(2)}, u32[]{:S(2)}) collective-permute-start(bf16[256,512]{1,0:T(8,128)(2,1)S(1)} %collective-permute-done), channel_id=1, source_target_pairs={{1,0},{2,1},{5,4},{6,5},{9,8},{10,9},{13,12},{14,13},{17,16},{18,1... | collective-permute-start | bytes 786440 | tf_op jit(solution)/shard_map/ppermute | solution.py:41
  170.2 11.9 %collective-permute-start.27 = (bf16[128,2048]{1,0:T(8,128)(2,1)S(1)}, bf16[128,2048]{1,0:T(8,128)(2,1)S(1)}, u32[]{:S(2)}, u32[]{:S(2)}) collective-permute-start(bf16[128,2048]{1,0:T(8,128)(2,1)S(1)} %pad_maximum_fusion.7), channel_id=1, source_target_pairs={{0,4},{1,5},{2,6},{3,7},{4,0},{5,1},{6,2},{7,3},{8,12},{9,13},{10,... | collective-permute-start | bytes 1572872 | tf_op jit(solution)/shard_map/ppermute | solution.py:41
  182.1 12.5 %collective-permute-start.17 = (bf16[256,512]{1,0:T(8,128)(2,1)S(1)}, bf16[256,512]{1,0:T(8,128)(2,1)S(1)}, u32[]{:S(2)}, u32[]{:S(2)}) collective-permute-start(bf16[256,512]{1,0:T(8,128)(2,1)S(1)} %collective-permute-done.16), channel_id=1, source_target_pairs={{1,2},{2,3},{5,6},{6,7},{9,10},{10,11},{13,14},{14,15},{17,18},{18... | collective-permute-start | bytes 786440 | tf_op jit(solution)/shard_map/ppermute | solution.py:41
  195.9 13.7 %collective-permute-start.9 = (bf16[256,512]{1,0:T(8,128)(2,1)S(1)}, bf16[256,512]{1,0:T(8,128)(2,1)S(1)}, u32[]{:S(2)}, u32[]{:S(2)}) collective-permute-start(bf16[256,512]{1,0:T(8,128)(2,1)S(1)} %collective-permute-done.8), channel_id=1, source_target_pairs={{2,3},{6,7},{10,11},{14,15},{18,19},{22,23},{26,27},{30,31},{34,35... | collective-permute-start | bytes 786440 | tf_op jit(solution)/shard_map/ppermute | solution.py:41
  213.1 13.7 %collective-permute-start.18 = (bf16[256,512]{1,0:T(8,128)(2,1)S(1)}, bf16[256,512]{1,0:T(8,128)(2,1)S(1)}, u32[]{:S(2)}, u32[]{:S(2)}) collective-permute-start(bf16[256,512]{1,0:T(8,128)(2,1)S(1)} %collective-permute-done.17), channel_id=1, source_target_pairs={{2,3},{6,7},{10,11},{14,15},{18,19},{22,23},{26,27},{30,31},{34,35... | collective-permute-start | bytes 786440 | tf_op jit(solution)/shard_map/ppermute | solution.py:41
  229.4 7.6 %collective-permute-done.20 = bf16[256,512]{1,0:T(8,128)(2,1)S(1)} collective-permute-done((bf16[256,512]{1,0:T(8,128)(2,1)S(1)}, bf16[256,512]{1,0:T(8,128)(2,1)S(1)}, u32[]{:S(2)}, u32[]{:S(2)}) %collective-permute-start.20) | collective-permute-done | bytes 262176 | tf_op jit(solution)/shard_map/ppermute | solution.py:41
  245.4 6.4 %conditional.4 = (bf16[256,2048]{1,0:T(8,128)(2,1)S(1)}, bf16[256,2048]{1,0:T(8,128)(2,1)}) conditional(s32[]{:T(128)} %convert_element_type.308, (bf16[256,512]{1,0:T(8,128)(2,1)S(1)}, bf16[256,512]{1,0:T(8,128)(2,1)S(1)}, bf16[256,512]{1,0:T(8,128)(2,1)S(1)}, bf16[512,2048]{1,0:T(8,128)(2,1)S(1)}) %tuple.100, (bf16[256,512]{1,0:T(8,128)(2,1)S(1)}, ...), branch_computations={%region_3.6_spmd, %region_6.0_spmd} | conditional | flops 2487745536 | bytes 23343120
  248.9 1.7 fusion.15
  251.8 1.9 slice.272
  253.7 1.9 collective-permute-start.49
  255.8 2.7 collective-permute-start.28
  260.6 3.4 collective-permute-start.50
  263.9 4.6 %collective-permute-start.51 = (bf16[32,2048]{1,0:T(8,128)(2,1)S(1)}, bf16[32,2048]{1,0:T(8,128)(2,1)S(1)}, u32[]{:S(2)}, u32[]{:S(2)}) collective-permute-start(bf16[32,2048]{1,0:T(8,128)(2,1)S(1)} %get-tuple-element.166), channel_id=1, source_target_pairs={{128,160},{129,161},{130,162},{131,163},{132,164},{133,165},{134,1... | collective-permute-start | bytes 393224 | tf_op jit(solution)/shard_map/ppermute | solution.py:41
  268.6 3.4 collective-permute-start.52
  273.0 2.5 collective-permute-done.52
  275.6 12.9 %collective-permute-start.53 = (bf16[16,2048]{1,0:T(8,128)(2,1)S(1)}, bf16[16,2048]{1,0:T(8,128)(2,1)S(1)}, u32[]{:S(2)}, u32[]{:S(2)}) collective-permute-start(bf16[16,2048]{1,0:T(8,128)(2,1)S(1)} %select_convert_fusion), channel_id=1, source_target_pairs={{128,192},{129,193},{130,194},{131,195},{132,196},{133,197},{134,1... | collective-permute-start | bytes 196616 | tf_op jit(solution)/shard_map/ppermute | solution.py:41
  288.7 3.7 collective-permute-start.29
  293.1 4.4 collective-permute-start.54
  297.5 4.0 collective-permute-start.55
  301.5 4.8 %collective-permute-start.56 = (bf16[16,512]{1,0:T(8,128)(2,1)S(1)}, bf16[16,512]{1,0:T(8,128)(2,1)S(1)}, u32[]{:S(2)}, u32[]{:S(2)}) collective-permute-start(bf16[16,512]{1,0:T(8,128)(2,1)S(1)} %get-tuple-element.175), channel_id=1, source_target_pairs={{128,131},{129,128},{130,129},{131,130},{132,135},{133,132},{134,1... | collective-permute-start | bytes 49160 | tf_op jit(solution)/shard_map/ppermute | solution.py:41
  309.4 12.5 %collective-permute-start.57 = (f32[16,512]{1,0:T(8,128)S(1)}, f32[16,512]{1,0:T(8,128)S(1)}, u32[]{:S(2)}, u32[]{:S(2)}) collective-permute-start(f32[16,512]{1,0:T(8,128)S(1)} %fusion.127), channel_id=1, source_target_pairs={{128,136},{129,137},{130,138},{131,139},{132,140},{133,141},{134,1... | collective-permute-start | bytes 98312 | tf_op jit(solution)/shard_map/ppermute | solution.py:41
  322.0 8.5 %collective-permute-done.57 = f32[16,512]{1,0:T(8,128)S(1)} collective-permute-done((f32[16,512]{1,0:T(8,128)S(1)}, f32[16,512]{1,0:T(8,128)S(1)}, u32[]{:S(2)}, u32[]{:S(2)}) %collective-permute-start.57) | collective-permute-done | bytes 32800 | tf_op jit(solution)/shard_map/ppermute | solution.py:41
  330.5 3.0 collective-permute-start.58
  333.5 3.4 collective-permute-start.59
  337.0 2.0 collective-permute-start.60
  340.3 4.3 collective-permute-done.60
  351.7 10.7 %collective-permute-done.40 = bf16[32,512]{1,0:T(8,128)(2,1)S(1)} collective-permute-done((bf16[32,512]{1,0:T(8,128)(2,1)S(1)}, bf16[32,512]{1,0:T(8,128)(2,1)S(1)}, u32[]{:S(2)}, u32[]{:S(2)}) %collective-permute-start.40) | collective-permute-done | bytes 32800 | tf_op jit(solution)/shard_map/ppermute | solution.py:41
  362.4 1.9 collective-permute-start.42
  364.3 1.9 collective-permute-start.43
  366.2 3.9 collective-permute-start.44
  372.2 2.2 collective-permute-done.44
  374.7 4.9 %collective-permute-start.45 = (bf16[32,2048]{1,0:T(8,128)(2,1)S(1)}, bf16[32,2048]{1,0:T(8,128)(2,1)S(1)}, u32[]{:S(2)}, u32[]{:S(2)}) collective-permute-start(bf16[32,2048]{1,0:T(8,128)(2,1)S(1)} %get-tuple-element.101), channel_id=1, source_target_pairs={{128,176},{129,177},{130,178},{131,179},{132,180},{133,181},{134,1... | collective-permute-start | bytes 393224 | tf_op jit(solution)/shard_map/ppermute | solution.py:41
  379.5 2.7 collective-permute-start.46
  382.3 2.8 collective-permute-start.47
  385.9 2.0 collective-permute-done.46
  387.9 2.5 collective-permute-done.47
  390.5 2.1 collective-permute-start.48
  392.8 1.6 collective-permute-done.48
  398.2 1.7 conditional.5
  400.1 1.7 collective-permute-start.67
  402.5 5.1 %collective-permute-done.67 = bf16[256,512]{1,0:T(8,128)(2,1)S(1)} collective-permute-done((bf16[256,512]{1,0:T(8,128)(2,1)S(1)}, bf16[256,512]{1,0:T(8,128)(2,1)S(1)}, u32[]{:S(2)}, u32[]{:S(2)}) %collective-permute-start.67) | collective-permute-done | bytes 262176 | tf_op jit(solution)/shard_map/ppermute | solution.py:41
  407.8 4.4 collective-permute-start.68
  413.8 3.9 collective-permute-start.74
  419.0 1.9 collective-permute-start.76
  421.1 4.8 %collective-permute-start.69 = (bf16[256,512]{1,0:T(8,128)(2,1)S(1)}, bf16[256,512]{1,0:T(8,128)(2,1)S(1)}, u32[]{:S(2)}, u32[]{:S(2)}) collective-permute-start(bf16[256,512]{1,0:T(8,128)(2,1)S(1)} %get-tuple-element.152), channel_id=1, source_target_pairs={{0,1},{1,2},{2,3},{4,5},{5,6},{6,7},{8,9},{9,10},{10,11},{12,13},{... | collective-permute-start | bytes 786440 | tf_op jit(solution)/shard_map/ppermute | solution.py:41
  427.3 2.5 collective-permute-done.69
  429.8 4.4 collective-permute-done.72
  434.4 6.8 %collective-permute-start.73 = (bf16[256,512]{1,0:T(8,128)(2,1)S(1)}, bf16[256,512]{1,0:T(8,128)(2,1)S(1)}, u32[]{:S(2)}, u32[]{:S(2)}) collective-permute-start(bf16[256,512]{1,0:T(8,128)(2,1)S(1)} %fusion.117), channel_id=1, source_target_pairs={{0,4},{1,5},{2,6},{3,7},{4,8},{5,9},{6,10},{7,11},{8,12},{9,13},{1... | collective-permute-start | bytes 786440 | tf_op jit(solution)/shard_map/ppermute | solution.py:41
  441.3 2.0 fusion.120
  443.3 13.3 %collective-permute-done.73 = bf16[256,512]{1,0:T(8,128)(2,1)S(1)} collective-permute-done((bf16[256,512]{1,0:T(8,128)(2,1)S(1)}, bf16[256,512]{1,0:T(8,128)(2,1)S(1)}, u32[]{:S(2)}, u32[]{:S(2)}) %collective-permute-start.73) | collective-permute-done | bytes 262176 | tf_op jit(solution)/shard_map/ppermute | solution.py:41
  (346 shorter events, 68.0 us)
Async XLA Ops:
  1.6 67.6 %collective-permute-start.21 = (bf16[32,512]{1,0:T(8,128)(2,1)S(1)}, bf16[32,512]{1,0:T(8,128)(2,1)S(1)}, u32[]{:S(2)}, u32[]{:S(2)}) collective-permute-start(bf16[32,512]{1,0:T(8,128)(2,1)S(1)} %constant_dynamic-slice_fusion), channel_id=1, source_target_pairs={{0,3},{1,0},{2,1},{3,2},{4,7},{5,4},{6,5},{7,6},{8,11},{9,8},{10,9... | collective-permute-start | bytes 98312 | tf_op jit(solution)/shard_map/ppermute | solution.py:41
  14.1 55.1 %collective-permute-start.22 = (bf16[32,512]{1,0:T(8,128)(2,1)S(1)}, bf16[32,512]{1,0:T(8,128)(2,1)S(1)}, u32[]{:S(2)}, u32[]{:S(2)}) collective-permute-start(bf16[32,512]{1,0:T(8,128)(2,1)S(1)} %constant_dynamic-slice_fusion), channel_id=1, source_target_pairs={{0,2},{1,3},{2,0},{3,1},{4,6},{5,7},{6,4},{7,5},{8,10},{9,11},{10,... | collective-permute-start | bytes 98312 | tf_op jit(solution)/shard_map/ppermute | solution.py:41
  27.4 15.1 %collective-permute-start.12 = (bf16[2,512]{1,0:T(2,128)(2,1)S(1)}, bf16[2,512]{1,0:T(2,128)(2,1)S(1)}, u32[]{:S(2)}, u32[]{:S(2)}) collective-permute-start(bf16[2,512]{1,0:T(2,128)(2,1)S(1)} %pad_maximum_fusion.11), channel_id=1, source_target_pairs={{0,3},{1,0},{2,1},{3,2},{4,7},{5,4},{6,5},{7,6},{8,11},{9,8},{10,9... | collective-permute-start | bytes 6152 | tf_op jit(solution)/shard_map/ppermute | solution.py:41
  31.5 21.4 %collective-permute-start.13 = (bf16[2,512]{1,0:T(2,128)(2,1)S(1)}, bf16[2,512]{1,0:T(2,128)(2,1)S(1)}, u32[]{:S(2)}, u32[]{:S(2)}) collective-permute-start(bf16[2,512]{1,0:T(2,128)(2,1)S(1)} %pad_maximum_fusion.11), channel_id=1, source_target_pairs={{0,2},{1,3},{2,0},{3,1},{4,6},{5,7},{6,4},{7,5},{8,10},{9,11},{10,... | collective-permute-start | bytes 6152 | tf_op jit(solution)/shard_map/ppermute | solution.py:41
  31.5 22.6 %collective-permute-start.14 = (bf16[2,512]{1,0:T(2,128)(2,1)S(1)}, bf16[2,512]{1,0:T(2,128)(2,1)S(1)}, u32[]{:S(2)}, u32[]{:S(2)}) collective-permute-start(bf16[2,512]{1,0:T(2,128)(2,1)S(1)} %pad_maximum_fusion.11), channel_id=1, source_target_pairs={{0,1},{1,2},{2,3},{3,0},{4,5},{5,6},{6,7},{7,4},{8,9},{9,10},{10,1... | collective-permute-start | bytes 6152 | tf_op jit(solution)/shard_map/ppermute | solution.py:41
  42.5 26.8 %collective-permute-start.23 = (bf16[32,512]{1,0:T(8,128)(2,1)S(1)}, bf16[32,512]{1,0:T(8,128)(2,1)S(1)}, u32[]{:S(2)}, u32[]{:S(2)}) collective-permute-start(bf16[32,512]{1,0:T(8,128)(2,1)S(1)} %constant_dynamic-slice_fusion), channel_id=1, source_target_pairs={{0,1},{1,2},{2,3},{3,0},{4,5},{5,6},{6,7},{7,4},{8,9},{9,10},{10,1... | collective-permute-start | bytes 98312 | tf_op jit(solution)/shard_map/ppermute | solution.py:41
  52.9 73.5 %collective-permute-start.6 = (bf16[256,512]{1,0:T(8,128)(2,1)S(1)}, bf16[256,512]{1,0:T(8,128)(2,1)}, u32[]{:S(2)}, u32[]{:S(2)}) collective-permute-start(bf16[256,512]{1,0:T(8,128)(2,1)S(1)} %get-tuple-element.169), channel_id=1, source_target_pairs={{1,0},{2,1},{3,2},{5,4},{6,5},{7,6},{9,8},{10,9},{11,10},{13,12},{... | collective-permute-start | bytes 786440 | tf_op jit(solution)/shard_map/ppermute | solution.py:41
  54.2 73.5 %collective-permute-start.7 = (bf16[256,512]{1,0:T(8,128)(2,1)S(1)}, bf16[256,512]{1,0:T(8,128)(2,1)}, u32[]{:S(2)}, u32[]{:S(2)}) collective-permute-start(bf16[256,512]{1,0:T(8,128)(2,1)S(1)} %get-tuple-element.169), channel_id=1, source_target_pairs={{0,1},{1,2},{2,3},{4,5},{5,6},{6,7},{8,9},{9,10},{10,11},{12,13},{... | collective-permute-start | bytes 786440 | tf_op jit(solution)/shard_map/ppermute | solution.py:41
  70.1 37.1 %collective-permute-start.24 = (bf16[32,2048]{1,0:T(8,128)(2,1)S(1)}, bf16[32,2048]{1,0:T(8,128)(2,1)S(1)}, u32[]{:S(2)}, u32[]{:S(2)}) collective-permute-start(bf16[32,2048]{1,0:T(8,128)(2,1)S(1)} %get-tuple-element.105), channel_id=1, source_target_pairs={{0,48},{1,49},{2,50},{3,51},{4,52},{5,53},{6,54},{7,55},{8,56},{9,... | collective-permute-start | bytes 393224 | tf_op jit(solution)/shard_map/ppermute | solution.py:41
  82.0 29.0 %collective-permute-start.25 = (bf16[32,2048]{1,0:T(8,128)(2,1)S(1)}, bf16[32,2048]{1,0:T(8,128)(2,1)S(1)}, u32[]{:S(2)}, u32[]{:S(2)}) collective-permute-start(bf16[32,2048]{1,0:T(8,128)(2,1)S(1)} %get-tuple-element.105), channel_id=1, source_target_pairs={{0,32},{1,33},{2,34},{3,35},{4,36},{5,37},{6,38},{7,39},{8,40},{9,... | collective-permute-start | bytes 393224 | tf_op jit(solution)/shard_map/ppermute | solution.py:41
  93.8 18.4 %collective-permute-start.26 = (bf16[32,2048]{1,0:T(8,128)(2,1)S(1)}, bf16[32,2048]{1,0:T(8,128)(2,1)S(1)}, u32[]{:S(2)}, u32[]{:S(2)}) collective-permute-start(bf16[32,2048]{1,0:T(8,128)(2,1)S(1)} %get-tuple-element.105), channel_id=1, source_target_pairs={{0,16},{1,17},{2,18},{3,19},{4,20},{5,21},{6,22},{7,23},{8,24},{9,... | collective-permute-start | bytes 393224 | tf_op jit(solution)/shard_map/ppermute | solution.py:41
  107.3 21.7 %collective-permute-start.1 = (bf16[256,512]{1,0:T(8,128)(2,1)S(1)}, bf16[256,512]{1,0:T(8,128)(2,1)S(1)}, u32[]{:S(2)}, u32[]{:S(2)}) collective-permute-start(bf16[256,512]{1,0:T(8,128)(2,1)S(1)} %get-tuple-element.167), channel_id=1, source_target_pairs={{0,1},{1,2},{2,3},{4,5},{5,6},{6,7},{8,9},{9,10},{10,11},{12,13},{... | collective-permute-start | bytes 786440 | tf_op jit(solution)/shard_map/ppermute | solution.py:41
  111.0 33.6 %collective-permute-start = (bf16[256,512]{1,0:T(8,128)(2,1)S(1)}, bf16[256,512]{1,0:T(8,128)(2,1)S(1)}, u32[]{:S(2)}, u32[]{:S(2)}) collective-permute-start(bf16[256,512]{1,0:T(8,128)(2,1)S(1)} %get-tuple-element.167), channel_id=1, source_target_pairs={{1,0},{2,1},{3,2},{5,4},{6,5},{7,6},{9,8},{10,9},{11,10},{13,12},{... | collective-permute-start | bytes 786440 | tf_op jit(solution)/shard_map/ppermute | solution.py:41
  112.3 44.8 %collective-permute-start.16 = (bf16[256,512]{1,0:T(8,128)(2,1)S(1)}, bf16[256,512]{1,0:T(8,128)(2,1)S(1)}, u32[]{:S(2)}, u32[]{:S(2)}) collective-permute-start(bf16[256,512]{1,0:T(8,128)(2,1)S(1)} %get-tuple-element.168), channel_id=1, source_target_pairs={{0,1},{1,2},{2,3},{4,5},{5,6},{6,7},{8,9},{9,10},{10,11},{12,13},{... | collective-permute-start | bytes 786440 | tf_op jit(solution)/shard_map/ppermute | solution.py:41
  126.4 43.8 %collective-permute-start.15 = (bf16[256,512]{1,0:T(8,128)(2,1)S(1)}, bf16[256,512]{1,0:T(8,128)(2,1)S(1)}, u32[]{:S(2)}, u32[]{:S(2)}) collective-permute-start(bf16[256,512]{1,0:T(8,128)(2,1)S(1)} %get-tuple-element.168), channel_id=1, source_target_pairs={{1,0},{2,1},{3,2},{5,4},{6,5},{7,6},{9,8},{10,9},{11,10},{13,12},{... | collective-permute-start | bytes 786440 | tf_op jit(solution)/shard_map/ppermute | solution.py:41
  127.7 54.4 %collective-permute-start.10 = (bf16[256,512]{1,0:T(8,128)(2,1)}, bf16[256,512]{1,0:T(8,128)(2,1)S(1)}, u32[]{:S(2)}, u32[]{:S(2)}) collective-permute-start(bf16[256,512]{1,0:T(8,128)(2,1)} %collective-permute-done.6), channel_id=1, source_target_pairs={{1,0},{2,1},{5,4},{6,5},{9,8},{10,9},{13,12},{14,13},{17,16},{18,1... | collective-permute-start | bytes 786440 | tf_op jit(solution)/shard_map/ppermute | solution.py:41
  129.0 65.6 %collective-permute-start.8 = (bf16[256,512]{1,0:T(8,128)(2,1)}, bf16[256,512]{1,0:T(8,128)(2,1)S(1)}, u32[]{:S(2)}, u32[]{:S(2)}) collective-permute-start(bf16[256,512]{1,0:T(8,128)(2,1)} %collective-permute-done.7), channel_id=1, source_target_pairs={{1,2},{2,3},{5,6},{6,7},{9,10},{10,11},{13,14},{14,15},{17,18},{18... | collective-permute-start | bytes 786440 | tf_op jit(solution)/shard_map/ppermute | solution.py:41
  144.5 51.4 %collective-permute-start.2 = (bf16[256,512]{1,0:T(8,128)(2,1)S(1)}, bf16[256,512]{1,0:T(8,128)(2,1)S(1)}, u32[]{:S(2)}, u32[]{:S(2)}) collective-permute-start(bf16[256,512]{1,0:T(8,128)(2,1)S(1)} %collective-permute-done.1), channel_id=1, source_target_pairs={{1,2},{2,3},{5,6},{6,7},{9,10},{10,11},{13,14},{14,15},{17,18},{18... | collective-permute-start | bytes 786440 | tf_op jit(solution)/shard_map/ppermute | solution.py:41
  157.1 52.6 %collective-permute-start.4 = (bf16[256,512]{1,0:T(8,128)(2,1)S(1)}, bf16[256,512]{1,0:T(8,128)(2,1)S(1)}, u32[]{:S(2)}, u32[]{:S(2)}) collective-permute-start(bf16[256,512]{1,0:T(8,128)(2,1)S(1)} %collective-permute-done), channel_id=1, source_target_pairs={{1,0},{2,1},{5,4},{6,5},{9,8},{10,9},{13,12},{14,13},{17,16},{18,1... | collective-permute-start | bytes 786440 | tf_op jit(solution)/shard_map/ppermute | solution.py:41
  170.2 42.8 %collective-permute-start.27 = (bf16[128,2048]{1,0:T(8,128)(2,1)S(1)}, bf16[128,2048]{1,0:T(8,128)(2,1)S(1)}, u32[]{:S(2)}, u32[]{:S(2)}) collective-permute-start(bf16[128,2048]{1,0:T(8,128)(2,1)S(1)} %pad_maximum_fusion.7), channel_id=1, source_target_pairs={{0,4},{1,5},{2,6},{3,7},{4,0},{5,1},{6,2},{7,3},{8,12},{9,13},{10,... | collective-permute-start | bytes 1572872 | tf_op jit(solution)/shard_map/ppermute | solution.py:41
  182.1 28.3 %collective-permute-start.17 = (bf16[256,512]{1,0:T(8,128)(2,1)S(1)}, bf16[256,512]{1,0:T(8,128)(2,1)S(1)}, u32[]{:S(2)}, u32[]{:S(2)}) collective-permute-start(bf16[256,512]{1,0:T(8,128)(2,1)S(1)} %collective-permute-done.16), channel_id=1, source_target_pairs={{1,2},{2,3},{5,6},{6,7},{9,10},{10,11},{13,14},{14,15},{17,18},{18... | collective-permute-start | bytes 786440 | tf_op jit(solution)/shard_map/ppermute | solution.py:41
  194.6 17.1 %collective-permute-start.19 = (bf16[256,512]{1,0:T(8,128)(2,1)S(1)}, bf16[256,512]{1,0:T(8,128)(2,1)S(1)}, u32[]{:S(2)}, u32[]{:S(2)}) collective-permute-start(bf16[256,512]{1,0:T(8,128)(2,1)S(1)} %collective-permute-done.15), channel_id=1, source_target_pairs={{1,0},{2,1},{5,4},{6,5},{9,8},{10,9},{13,12},{14,13},{17,16},{18,1... | collective-permute-start | bytes 786440 | tf_op jit(solution)/shard_map/ppermute | solution.py:41
  195.9 30.9 %collective-permute-start.9 = (bf16[256,512]{1,0:T(8,128)(2,1)S(1)}, bf16[256,512]{1,0:T(8,128)(2,1)S(1)}, u32[]{:S(2)}, u32[]{:S(2)}) collective-permute-start(bf16[256,512]{1,0:T(8,128)(2,1)S(1)} %collective-permute-done.8), channel_id=1, source_target_pairs={{2,3},{6,7},{10,11},{14,15},{18,19},{22,23},{26,27},{30,31},{34,35... | collective-permute-start | bytes 786440 | tf_op jit(solution)/shard_map/ppermute | solution.py:41
  209.6 19.7 %collective-permute-start.3 = (bf16[256,512]{1,0:T(8,128)(2,1)S(1)}, bf16[256,512]{1,0:T(8,128)(2,1)S(1)}, u32[]{:S(2)}, u32[]{:S(2)}) collective-permute-start(bf16[256,512]{1,0:T(8,128)(2,1)S(1)} %collective-permute-done.2), channel_id=1, source_target_pairs={{2,3},{6,7},{10,11},{14,15},{18,19},{22,23},{26,27},{30,31},{34,35... | collective-permute-start | bytes 786440 | tf_op jit(solution)/shard_map/ppermute | solution.py:41
  210.4 27.0 %collective-permute-start.11 = (bf16[256,512]{1,0:T(8,128)(2,1)S(1)}, bf16[256,512]{1,0:T(8,128)(2,1)S(1)}, u32[]{:S(2)}, u32[]{:S(2)}) collective-permute-start(bf16[256,512]{1,0:T(8,128)(2,1)S(1)} %collective-permute-done.10), channel_id=1, source_target_pairs={{1,0},{5,4},{9,8},{13,12},{17,16},{21,20},{25,24},{29,28},{33,32},... | collective-permute-start | bytes 786440 | tf_op jit(solution)/shard_map/ppermute | solution.py:41
  211.7 25.8 %collective-permute-start.5 = (bf16[256,512]{1,0:T(8,128)(2,1)S(1)}, bf16[256,512]{1,0:T(8,128)(2,1)S(1)}, u32[]{:S(2)}, u32[]{:S(2)}) collective-permute-start(bf16[256,512]{1,0:T(8,128)(2,1)S(1)} %collective-permute-done.4), channel_id=1, source_target_pairs={{1,0},{5,4},{9,8},{13,12},{17,16},{21,20},{25,24},{29,28},{33,32},... | collective-permute-start | bytes 786440 | tf_op jit(solution)/shard_map/ppermute | solution.py:41
  213.1 16.3 %collective-permute-start.18 = (bf16[256,512]{1,0:T(8,128)(2,1)S(1)}, bf16[256,512]{1,0:T(8,128)(2,1)S(1)}, u32[]{:S(2)}, u32[]{:S(2)}) collective-permute-start(bf16[256,512]{1,0:T(8,128)(2,1)S(1)} %collective-permute-done.17), channel_id=1, source_target_pairs={{2,3},{6,7},{10,11},{14,15},{18,19},{22,23},{26,27},{30,31},{34,35... | collective-permute-start | bytes 786440 | tf_op jit(solution)/shard_map/ppermute | solution.py:41
  226.8 10.3 %collective-permute-start.20 = (bf16[256,512]{1,0:T(8,128)(2,1)S(1)}, bf16[256,512]{1,0:T(8,128)(2,1)S(1)}, u32[]{:S(2)}, u32[]{:S(2)}) collective-permute-start(bf16[256,512]{1,0:T(8,128)(2,1)S(1)} %collective-permute-done.19), channel_id=1, source_target_pairs={{1,0},{5,4},{9,8},{13,12},{17,16},{21,20},{25,24},{29,28},{33,32},... | collective-permute-start | bytes 786440 | tf_op jit(solution)/shard_map/ppermute | solution.py:41
  255.8 32.8 %collective-permute-start.28 = (bf16[256,512]{1,0:T(8,128)(2,1)S(1)}, bf16[256,512]{1,0:T(8,128)(2,1)S(1)}, u32[]{:S(2)}, u32[]{:S(2)}) collective-permute-start(bf16[256,512]{1,0:T(8,128)(2,1)S(1)} %get-tuple-element.162), channel_id=1, source_target_pairs={{0,1},{4,5},{8,9},{12,13},{16,17},{20,21},{24,25},{28,29},{32,33},... | collective-permute-start | bytes 786440 | tf_op jit(solution)/shard_map/ppermute | solution.py:41
  258.5 30.1 %collective-permute-start.31 = (bf16[256,512]{1,0:T(8,128)(2,1)S(1)}, bf16[256,512]{1,0:T(8,128)(2,1)S(1)}, u32[]{:S(2)}, u32[]{:S(2)}) collective-permute-start(bf16[256,512]{1,0:T(8,128)(2,1)S(1)} %get-tuple-element.163), channel_id=1, source_target_pairs={{3,2},{7,6},{11,10},{15,14},{19,18},{23,22},{27,26},{31,30},{35,34... | collective-permute-start | bytes 786440 | tf_op jit(solution)/shard_map/ppermute | solution.py:41
  260.6 12.2 %collective-permute-start.50 = (bf16[32,2048]{1,0:T(8,128)(2,1)S(1)}, bf16[32,2048]{1,0:T(8,128)(2,1)S(1)}, u32[]{:S(2)}, u32[]{:S(2)}) collective-permute-start(bf16[32,2048]{1,0:T(8,128)(2,1)S(1)} %get-tuple-element.164), channel_id=1, source_target_pairs={{128,144},{129,145},{130,146},{131,147},{132,148},{133,149},{134,1... | collective-permute-start | bytes 393224 | tf_op jit(solution)/shard_map/ppermute | solution.py:41
  263.9 9.1 %collective-permute-start.51 = (bf16[32,2048]{1,0:T(8,128)(2,1)S(1)}, bf16[32,2048]{1,0:T(8,128)(2,1)S(1)}, u32[]{:S(2)}, u32[]{:S(2)}) collective-permute-start(bf16[32,2048]{1,0:T(8,128)(2,1)S(1)} %get-tuple-element.166), channel_id=1, source_target_pairs={{128,160},{129,161},{130,162},{131,163},{132,164},{133,165},{134,1... | collective-permute-start | bytes 393224 | tf_op jit(solution)/shard_map/ppermute | solution.py:41
  275.6 17.4 %collective-permute-start.53 = (bf16[16,2048]{1,0:T(8,128)(2,1)S(1)}, bf16[16,2048]{1,0:T(8,128)(2,1)S(1)}, u32[]{:S(2)}, u32[]{:S(2)}) collective-permute-start(bf16[16,2048]{1,0:T(8,128)(2,1)S(1)} %select_convert_fusion), channel_id=1, source_target_pairs={{128,192},{129,193},{130,194},{131,195},{132,196},{133,197},{134,1... | collective-permute-start | bytes 196616 | tf_op jit(solution)/shard_map/ppermute | solution.py:41
  288.7 17.6 %collective-permute-start.29 = (bf16[256,512]{1,0:T(8,128)(2,1)S(1)}, bf16[256,512]{1,0:T(8,128)(2,1)S(1)}, u32[]{:S(2)}, u32[]{:S(2)}) collective-permute-start(bf16[256,512]{1,0:T(8,128)(2,1)S(1)} %get-tuple-element.160), channel_id=1, source_target_pairs={{0,1},{1,2},{4,5},{5,6},{8,9},{9,10},{12,13},{13,14},{16,17},{17,1... | collective-permute-start | bytes 786440 | tf_op jit(solution)/shard_map/ppermute | solution.py:41
  292.4 14.0 %collective-permute-start.32 = (bf16[256,512]{1,0:T(8,128)(2,1)S(1)}, bf16[256,512]{1,0:T(8,128)(2,1)S(1)}, u32[]{:S(2)}, u32[]{:S(2)}) collective-permute-start(bf16[256,512]{1,0:T(8,128)(2,1)S(1)} %get-tuple-element.161), channel_id=1, source_target_pairs={{2,1},{3,2},{6,5},{7,6},{10,9},{11,10},{14,13},{15,14},{18,17},{19... | collective-permute-start | bytes 786440 | tf_op jit(solution)/shard_map/ppermute | solution.py:41
  293.1 16.2 %collective-permute-start.54 = (bf16[16,512]{1,0:T(8,128)(2,1)S(1)}, bf16[16,512]{1,0:T(8,128)(2,1)S(1)}, u32[]{:S(2)}, u32[]{:S(2)}) collective-permute-start(bf16[16,512]{1,0:T(8,128)(2,1)S(1)} %get-tuple-element.174), channel_id=1, source_target_pairs={{128,129},{129,130},{130,131},{131,128},{132,133},{133,134},{134,1... | collective-permute-start | bytes 49160 | tf_op jit(solution)/shard_map/ppermute | solution.py:41
  297.5 11.8 %collective-permute-start.55 = (bf16[16,512]{1,0:T(8,128)(2,1)S(1)}, bf16[16,512]{1,0:T(8,128)(2,1)S(1)}, u32[]{:S(2)}, u32[]{:S(2)}) collective-permute-start(bf16[16,512]{1,0:T(8,128)(2,1)S(1)} %get-tuple-element.176), channel_id=1, source_target_pairs={{128,130},{129,131},{130,128},{131,129},{132,134},{133,135},{134,1... | collective-permute-start | bytes 49160 | tf_op jit(solution)/shard_map/ppermute | solution.py:41
  301.5 7.8 %collective-permute-start.56 = (bf16[16,512]{1,0:T(8,128)(2,1)S(1)}, bf16[16,512]{1,0:T(8,128)(2,1)S(1)}, u32[]{:S(2)}, u32[]{:S(2)}) collective-permute-start(bf16[16,512]{1,0:T(8,128)(2,1)S(1)} %get-tuple-element.175), channel_id=1, source_target_pairs={{128,131},{129,128},{130,129},{131,130},{132,135},{133,132},{134,1... | collective-permute-start | bytes 49160 | tf_op jit(solution)/shard_map/ppermute | solution.py:41
  306.6 32.5 %collective-permute-start.30 = (bf16[256,512]{1,0:T(8,128)(2,1)S(1)}, bf16[256,512]{1,0:T(8,128)(2,1)S(1)}, u32[]{:S(2)}, u32[]{:S(2)}) collective-permute-start(bf16[256,512]{1,0:T(8,128)(2,1)S(1)} %get-tuple-element.158), channel_id=1, source_target_pairs={{0,1},{1,2},{2,3},{4,5},{5,6},{6,7},{8,9},{9,10},{10,11},{12,13},{... | collective-permute-start | bytes 786440 | tf_op jit(solution)/shard_map/ppermute | solution.py:41
  308.0 31.1 %collective-permute-start.33 = (bf16[256,512]{1,0:T(8,128)(2,1)S(1)}, bf16[256,512]{1,0:T(8,128)(2,1)S(1)}, u32[]{:S(2)}, u32[]{:S(2)}) collective-permute-start(bf16[256,512]{1,0:T(8,128)(2,1)S(1)} %get-tuple-element.159), channel_id=1, source_target_pairs={{1,0},{2,1},{3,2},{5,4},{6,5},{7,6},{9,8},{10,9},{11,10},{13,12},{... | collective-permute-start | bytes 786440 | tf_op jit(solution)/shard_map/ppermute | solution.py:41
  309.4 21.1 %collective-permute-start.57 = (f32[16,512]{1,0:T(8,128)S(1)}, f32[16,512]{1,0:T(8,128)S(1)}, u32[]{:S(2)}, u32[]{:S(2)}) collective-permute-start(f32[16,512]{1,0:T(8,128)S(1)} %fusion.127), channel_id=1, source_target_pairs={{128,136},{129,137},{130,138},{131,139},{132,140},{133,141},{134,1... | collective-permute-start | bytes 98312 | tf_op jit(solution)/shard_map/ppermute | solution.py:41
  330.5 9.5 %collective-permute-start.58 = (f32[16,512]{1,0:T(8,128)S(1)}, f32[16,512]{1,0:T(8,128)S(1)}, u32[]{:S(2)}, u32[]{:S(2)}) collective-permute-start(f32[16,512]{1,0:T(8,128)S(1)} %add.262), channel_id=1, source_target_pairs={{128,131},{129,128},{130,129},{131,130},{132,135},{133,132},{134,1... | collective-permute-start | bytes 98312 | tf_op jit(solution)/shard_map/ppermute | solution.py:41
  337.0 7.6 %collective-permute-start.60 = (f32[16,512]{1,0:T(8,128)S(1)}, f32[16,512]{1,0:T(8,128)S(1)}, u32[]{:S(2)}, u32[]{:S(2)}) collective-permute-start(f32[16,512]{1,0:T(8,128)S(1)} %add.262), channel_id=1, source_target_pairs={{128,129},{129,130},{130,131},{131,128},{132,133},{133,134},{134,1... | collective-permute-start | bytes 98312 | tf_op jit(solution)/shard_map/ppermute | solution.py:41
  347.6 22.6 %collective-permute-start.62 = (bf16[16,2048]{1,0:T(8,128)(2,1)S(1)}, bf16[16,2048]{1,0:T(8,128)(2,1)S(1)}, u32[]{:S(2)}, u32[]{:S(2)}) collective-permute-start(bf16[16,2048]{1,0:T(8,128)(2,1)S(1)} %subtract_convert_fusion.1), channel_id=1, source_target_pairs={{200,72},{201,73},{202,74},{203,75},{204,76},{205,77},{206,78},{20... | collective-permute-start | bytes 196616 | tf_op jit(solution)/shard_map/ppermute | solution.py:41
  349.7 12.7 %collective-permute-start.40 = (bf16[32,512]{1,0:T(8,128)(2,1)S(1)}, bf16[32,512]{1,0:T(8,128)(2,1)S(1)}, u32[]{:S(2)}, u32[]{:S(2)}) collective-permute-start(bf16[32,512]{1,0:T(8,128)(2,1)S(1)} %fusion.131), channel_id=1, source_target_pairs={{72,192},{73,193},{74,194},{75,195},{76,196},{77,197},{78,198},{79... | collective-permute-start | bytes 98312 | tf_op jit(solution)/shard_map/ppermute | solution.py:41
  351.0 11.4 %collective-permute-start.41 = (bf16[32,512]{1,0:T(8,128)(2,1)S(1)}, bf16[32,512]{1,0:T(8,128)(2,1)S(1)}, u32[]{:S(2)}, u32[]{:S(2)}) collective-permute-start(bf16[32,512]{1,0:T(8,128)(2,1)S(1)} %fusion.131), channel_id=1, source_target_pairs={{72,200},{73,201},{74,202},{75,203},{76,204},{77,205},{78,206},{79... | collective-permute-start | bytes 98312 | tf_op jit(solution)/shard_map/ppermute | solution.py:41
  362.4 9.2 %collective-permute-start.42 = (bf16[32,512]{1,0:T(8,128)(2,1)S(1)}, bf16[32,512]{1,0:T(8,128)(2,1)S(1)}, u32[]{:S(2)}, u32[]{:S(2)}) collective-permute-start(bf16[32,512]{1,0:T(8,128)(2,1)S(1)} %add_add_fusion), channel_id=1, source_target_pairs={{128,131},{129,128},{130,129},{131,130},{132,135},{133,132},{134,1... | collective-permute-start | bytes 98312 | tf_op jit(solution)/shard_map/ppermute | solution.py:41
  364.3 7.9 %collective-permute-start.43 = (bf16[32,512]{1,0:T(8,128)(2,1)S(1)}, bf16[32,512]{1,0:T(8,128)(2,1)S(1)}, u32[]{:S(2)}, u32[]{:S(2)}) collective-permute-start(bf16[32,512]{1,0:T(8,128)(2,1)S(1)} %add_add_fusion), channel_id=1, source_target_pairs={{128,130},{129,131},{130,128},{131,129},{132,134},{133,135},{134,1... | collective-permute-start | bytes 98312 | tf_op jit(solution)/shard_map/ppermute | solution.py:41
  366.2 8.2 %collective-permute-start.44 = (bf16[32,512]{1,0:T(8,128)(2,1)S(1)}, bf16[32,512]{1,0:T(8,128)(2,1)S(1)}, u32[]{:S(2)}, u32[]{:S(2)}) collective-permute-start(bf16[32,512]{1,0:T(8,128)(2,1)S(1)} %add_add_fusion), channel_id=1, source_target_pairs={{128,129},{129,130},{130,131},{131,128},{132,133},{133,134},{134,1... | collective-permute-start | bytes 98312 | tf_op jit(solution)/shard_map/ppermute | solution.py:41
  370.2 12.1 %collective-permute-start.63 = (bf16[32,2048]{1,0:T(8,128)(2,1)S(1)}, bf16[32,2048]{1,0:T(8,128)(2,1)S(1)}, u32[]{:S(2)}, u32[]{:S(2)}) collective-permute-start(bf16[32,2048]{1,0:T(8,128)(2,1)S(1)} %constant_dynamic-update-slice_fusion.10), channel_id=1, source_target_pairs={{72,120},{73,121},{74,122},{75,123},{76,124},{77,125},{78,126},{79... | collective-permute-start | bytes 393224 | tf_op jit(solution)/shard_map/ppermute | solution.py:41
  370.9 14.2 %collective-permute-start.64 = (bf16[32,2048]{1,0:T(8,128)(2,1)S(1)}, bf16[32,2048]{1,0:T(8,128)(2,1)S(1)}, u32[]{:S(2)}, u32[]{:S(2)}) collective-permute-start(bf16[32,2048]{1,0:T(8,128)(2,1)S(1)} %constant_dynamic-update-slice_fusion.10), channel_id=1, source_target_pairs={{88,120},{89,121},{90,122},{91,123},{92,124},{93,125},{94,126},{95... | collective-permute-start | bytes 393224 | tf_op jit(solution)/shard_map/ppermute | solution.py:41
  371.6 13.5 %collective-permute-start.65 = (bf16[32,2048]{1,0:T(8,128)(2,1)S(1)}, bf16[32,2048]{1,0:T(8,128)(2,1)S(1)}, u32[]{:S(2)}, u32[]{:S(2)}) collective-permute-start(bf16[32,2048]{1,0:T(8,128)(2,1)S(1)} %constant_dynamic-update-slice_fusion.10), channel_id=1, source_target_pairs={{104,120},{105,121},{106,122},{107,123},{108,124},{109,125},{110,1... | collective-permute-start | bytes 393224 | tf_op jit(solution)/shard_map/ppermute | solution.py:41
  374.7 11.2 %collective-permute-start.45 = (bf16[32,2048]{1,0:T(8,128)(2,1)S(1)}, bf16[32,2048]{1,0:T(8,128)(2,1)S(1)}, u32[]{:S(2)}, u32[]{:S(2)}) collective-permute-start(bf16[32,2048]{1,0:T(8,128)(2,1)S(1)} %get-tuple-element.101), channel_id=1, source_target_pairs={{128,176},{129,177},{130,178},{131,179},{132,180},{133,181},{134,1... | collective-permute-start | bytes 393224 | tf_op jit(solution)/shard_map/ppermute | solution.py:41
  379.5 8.4 %collective-permute-start.46 = (bf16[32,2048]{1,0:T(8,128)(2,1)S(1)}, bf16[32,2048]{1,0:T(8,128)(2,1)S(1)}, u32[]{:S(2)}, u32[]{:S(2)}) collective-permute-start(bf16[32,2048]{1,0:T(8,128)(2,1)S(1)} %get-tuple-element.101), channel_id=1, source_target_pairs={{128,160},{129,161},{130,162},{131,163},{132,164},{133,165},{134,1... | collective-permute-start | bytes 393224 | tf_op jit(solution)/shard_map/ppermute | solution.py:41
  382.3 8.1 %collective-permute-start.47 = (bf16[32,2048]{1,0:T(8,128)(2,1)S(1)}, bf16[32,2048]{1,0:T(8,128)(2,1)S(1)}, u32[]{:S(2)}, u32[]{:S(2)}) collective-permute-start(bf16[32,2048]{1,0:T(8,128)(2,1)S(1)} %get-tuple-element.101), channel_id=1, source_target_pairs={{128,144},{129,145},{130,146},{131,147},{132,148},{133,149},{134,1... | collective-permute-start | bytes 393224 | tf_op jit(solution)/shard_map/ppermute | solution.py:41
  400.1 7.6 %collective-permute-start.67 = (bf16[256,512]{1,0:T(8,128)(2,1)S(1)}, bf16[256,512]{1,0:T(8,128)(2,1)S(1)}, u32[]{:S(2)}, u32[]{:S(2)}) collective-permute-start(bf16[256,512]{1,0:T(8,128)(2,1)S(1)} %get-tuple-element.156), channel_id=1, source_target_pairs={{0,1},{4,5},{8,9},{12,13},{16,17},{20,21},{24,25},{28,29},{32,33},... | collective-permute-start | bytes 786440 | tf_op jit(solution)/shard_map/ppermute | solution.py:41
  407.8 13.2 %collective-permute-start.68 = (bf16[256,512]{1,0:T(8,128)(2,1)S(1)}, bf16[256,512]{1,0:T(8,128)(2,1)S(1)}, u32[]{:S(2)}, u32[]{:S(2)}) collective-permute-start(bf16[256,512]{1,0:T(8,128)(2,1)S(1)} %get-tuple-element.154), channel_id=1, source_target_pairs={{0,1},{1,2},{4,5},{5,6},{8,9},{9,10},{12,13},{13,14},{16,17},{17,1... | collective-permute-start | bytes 786440 | tf_op jit(solution)/shard_map/ppermute | solution.py:41
  412.2 8.8 %collective-permute-start.71 = (bf16[256,512]{1,0:T(8,128)(2,1)S(1)}, bf16[256,512]{1,0:T(8,128)(2,1)S(1)}, u32[]{:S(2)}, u32[]{:S(2)}) collective-permute-start(bf16[256,512]{1,0:T(8,128)(2,1)S(1)} %get-tuple-element.155), channel_id=1, source_target_pairs={{2,1},{3,2},{6,5},{7,6},{10,9},{11,10},{14,13},{15,14},{18,17},{19... | collective-permute-start | bytes 786440 | tf_op jit(solution)/shard_map/ppermute | solution.py:41
  413.8 13.5 %collective-permute-start.74 = (f32[2,128]{1,0:T(2,128)S(1)}, f32[2,128]{1,0:T(2,128)S(1)}, u32[]{:S(2)}, u32[]{:S(2)}) collective-permute-start(f32[2,128]{1,0:T(2,128)S(1)} %bitcast.154), channel_id=1, source_target_pairs={{0,3},{1,0},{2,1},{3,2},{4,7},{5,4},{6,5},{7,6},{8,11},{9,8},{10,9... | collective-permute-start | bytes 3080 | tf_op jit(solution)/shard_map/ppermute | solution.py:41
  417.8 9.5 %collective-permute-start.75 = (f32[2,128]{1,0:T(2,128)S(1)}, f32[2,128]{1,0:T(2,128)S(1)}, u32[]{:S(2)}, u32[]{:S(2)}) collective-permute-start(f32[2,128]{1,0:T(2,128)S(1)} %bitcast.155), channel_id=1, source_target_pairs={{0,2},{1,3},{2,0},{3,1},{4,6},{5,7},{6,4},{7,5},{8,10},{9,11},{10,... | collective-permute-start | bytes 3080 | tf_op jit(solution)/shard_map/ppermute | solution.py:41
  419.0 8.3 %collective-permute-start.76 = (f32[2,128]{1,0:T(2,128)S(1)}, f32[2,128]{1,0:T(2,128)S(1)}, u32[]{:S(2)}, u32[]{:S(2)}) collective-permute-start(f32[2,128]{1,0:T(2,128)S(1)} %bitcast.156), channel_id=1, source_target_pairs={{0,1},{1,2},{2,3},{3,0},{4,5},{5,6},{6,7},{7,4},{8,9},{9,10},{10,1... | collective-permute-start | bytes 3080 | tf_op jit(solution)/shard_map/ppermute | solution.py:41
  421.1 8.7 %collective-permute-start.69 = (bf16[256,512]{1,0:T(8,128)(2,1)S(1)}, bf16[256,512]{1,0:T(8,128)(2,1)S(1)}, u32[]{:S(2)}, u32[]{:S(2)}) collective-permute-start(bf16[256,512]{1,0:T(8,128)(2,1)S(1)} %get-tuple-element.152), channel_id=1, source_target_pairs={{0,1},{1,2},{2,3},{4,5},{5,6},{6,7},{8,9},{9,10},{10,11},{12,13},{... | collective-permute-start | bytes 786440 | tf_op jit(solution)/shard_map/ppermute | solution.py:41
  426.0 8.3 %collective-permute-start.72 = (bf16[256,512]{1,0:T(8,128)(2,1)S(1)}, bf16[256,512]{1,0:T(8,128)(2,1)S(1)}, u32[]{:S(2)}, u32[]{:S(2)}) collective-permute-start(bf16[256,512]{1,0:T(8,128)(2,1)S(1)} %get-tuple-element.153), channel_id=1, source_target_pairs={{1,0},{2,1},{3,2},{5,4},{6,5},{7,6},{9,8},{10,9},{11,10},{13,12},{... | collective-permute-start | bytes 786440 | tf_op jit(solution)/shard_map/ppermute | solution.py:41
  434.4 22.2 %collective-permute-start.73 = (bf16[256,512]{1,0:T(8,128)(2,1)S(1)}, bf16[256,512]{1,0:T(8,128)(2,1)S(1)}, u32[]{:S(2)}, u32[]{:S(2)}) collective-permute-start(bf16[256,512]{1,0:T(8,128)(2,1)S(1)} %fusion.117), channel_id=1, source_target_pairs={{0,4},{1,5},{2,6},{3,7},{4,8},{5,9},{6,10},{7,11},{8,12},{9,13},{1... | collective-permute-start | bytes 786440 | tf_op jit(solution)/shard_map/ppermute | solution.py:41
  (83 other events, 1236.8 us)
